TPU v7x, 512 devices: a whole 4x4x16 slice. The times are simulated.
512 devices in a mesh: row: 32 (over x, y, core), col: 16 (over z).
Axes of the slice: x: 4, y: 4, z: 16, core: 2. Of those that a mesh axis runs over, the one named last changes fastest.
Arguments:
- inputs: bfloat16 [2048, 6144], P('row', 'col'), may hold values from -6 to 6
- out_grad: bfloat16 [2048, 6144], P('row', 'col'), may hold values from -6 to 6
- preact: bfloat16 [2048, 12288], P('col', 'row'), may hold values from -6 to 6
- weight_in: bfloat16 [6144, 12288], P('col', 'row'), may hold values from -0.078125 to 0.078125
- weight_out: bfloat16 [12288, 6144], P('row', 'col'), may hold values from -0.0546875 to 0.0546875
- moment_in: bfloat16 [6144, 12288], P('col', 'row'), may hold values from -3 to 3
- second_in: bfloat16 [6144, 12288], P('col', 'row'), may hold values from 0.049804688 to 5
- moment_out: bfloat16 [12288, 6144], P('row', 'col'), may hold values from -3 to 3
- second_out: bfloat16 [12288, 6144], P('row', 'col'), may hold values from 0.049804688 to 5
Outputs:
- input_grad: bfloat16 [2048, 6144], P('row', 'col')
- new_weight_in: bfloat16 [6144, 12288], P('col', 'row')
- new_moment_in: bfloat16 [6144, 12288], P('col', 'row')
- new_second_in: bfloat16 [6144, 12288], P('col', 'row')
- new_weight_out: bfloat16 [12288, 6144], P('row', 'col')
- new_moment_out: bfloat16 [12288, 6144], P('row', 'col')
- new_second_out: bfloat16 [12288, 6144], P('row', 'col')
All inputs are finite; a program needn't handle non-finite values.
Results may differ from a plain program's by a relative error of at most 0.03.
Values may be sent and summed in bfloat16 or wider, within the bound.
A program may use at most 64 MiB of HBM per device.

v0:
```python
import jax
import jax.numpy as jnp
from jax import lax
from jax.sharding import PartitionSpec as P

gelu_coef = 0.7978845608
beta_first = 0.9
beta_second = 0.95
learn_rate = 0.003
epsilon_adam = 1e-08
correct_first = 1.0 - 0.9**10
correct_second = 1.0 - 0.95**10


def gelu_parts(preact):
    values = preact.astype(jnp.float32)
    tangent = jnp.tanh(gelu_coef * (values + 0.044715 * values * values * values))
    activated = 0.5 * values * (1.0 + tangent)
    slopes = 0.5 * (1.0 + tangent) + 0.5 * values * (1.0 - tangent * tangent) * gelu_coef * (
        1.0 + 3.0 * 0.044715 * values * values
    )
    return (activated, slopes)


def adam_step(weight, moment, second, grads):
    first_new = beta_first * moment.astype(jnp.float32) + (1.0 - beta_first) * grads
    second_new = beta_second * second.astype(jnp.float32) + (1.0 - beta_second) * grads * grads
    weight_new = weight.astype(jnp.float32) - learn_rate * (first_new / correct_first) / (
        jnp.sqrt(second_new / correct_second) + epsilon_adam
    )
    return (
        weight_new.astype(jnp.bfloat16),
        first_new.astype(jnp.bfloat16),
        second_new.astype(jnp.bfloat16),
    )


def shards(
    inputs, out_grad, preact, weight_in, weight_out, moment_in, second_in, moment_out, second_out
):
    rows_grad = lax.all_gather(out_grad, "row", axis=0, tiled=True)
    picked = rows_grad
    shared = lax.psum_scatter(
        lax.dot_general(
            picked, weight_out, (((1,), (1,)), ((), ())), preferred_element_type=jnp.float32
        ).astype(jnp.bfloat16),
        "col",
        scatter_dimension=0,
        tiled=True,
    ).astype(jnp.float32)
    activated, slopes = gelu_parts(preact)
    act_all, delta_all = (
        lax.all_gather(activated.astype(jnp.bfloat16), "col", axis=0, tiled=True),
        lax.all_gather((shared * slopes).astype(jnp.bfloat16), "col", axis=0, tiled=True),
    )
    rows_in = lax.all_gather(inputs, "row", axis=0, tiled=True)
    grad_out = lax.dot_general(
        act_all, rows_grad, (((0,), (0,)), ((), ())), preferred_element_type=jnp.float32
    )
    grad_in = lax.dot_general(
        rows_in, delta_all, (((0,), (0,)), ((), ())), preferred_element_type=jnp.float32
    )
    picked = delta_all
    input_grad = lax.psum_scatter(
        lax.dot_general(
            picked, weight_in, (((1,), (1,)), ((), ())), preferred_element_type=jnp.float32
        ).astype(jnp.bfloat16),
        "row",
        scatter_dimension=0,
        tiled=True,
    )
    weight_a, moment_a, second_a = adam_step(weight_in, moment_in, second_in, grad_in)
    weight_b, moment_b, second_b = adam_step(weight_out, moment_out, second_out, grad_out)
    return (input_grad, weight_a, moment_a, second_a, weight_b, moment_b, second_b)


def solution(mesh):
    placed = (
        P("row", "col"),
        P("row", "col"),
        P("col", "row"),
        P("col", "row"),
        P("row", "col"),
        P("col", "row"),
        P("col", "row"),
        P("row", "col"),
        P("row", "col"),
    )
    return jax.shard_map(
        shards,
        mesh=mesh,
        in_specs=placed,
        out_specs=(
            P("row", "col"),
            P("col", "row"),
            P("col", "row"),
            P("col", "row"),
            P("row", "col"),
            P("row", "col"),
            P("row", "col"),
        ),
        check_vma=False,
    )
```

profile of v0, /device:TPU:6, one launch (start us, length us, event | category | flops | bytes accessed | tf_op | source)
XLA Modules:
  0.0 465.3 jit_solution(15268040868537862878)
XLA Ops:
  7.2 0.0 all-gather.5.cloned.1.call-start
  7.2 0.7 all-gather.5.cloned.1.call-update
  7.9 0.0 reduce-scatter.3.cloned.1.call-start
  7.9 65.8 %all-gather.5.cloned.1.call-done = bf16[2048,384]{1,0:T(8,128)(2,1)} async-done(((bf16[64,384]{1,0:T(8,128)(2,1)}), bf16[2048,384]{1,0:T(8,128)(2,1)}) %all-gather.5.cloned.1.call-update) | async-done | bytes 1572880 | tf_op jit(solution)/shard_map/all_gather | solution.py:41
  73.8 3.7 convolution_convert_fusion.1
  77.5 0.0 copy-start.8
  77.5 0.0 copy-start.2
  77.5 0.0 reduce-scatter.3.cloned.1.call-update
  77.5 0.0 all-gather.7.cloned.1.call-start
  77.6 71.7 %reduce-scatter.3.cloned.1.call-done = bf16[128,384]{1,0:T(8,128)(2,1)} async-done(((bf16[2048,384]{1,0:T(8,128)(2,1)}), bf16[128,384]{1,0:T(8,128)(2,1)}) %reduce-scatter.3.cloned.1.call-update) | async-done | bytes 98320 | tf_op jit(solution)/shard_map/reduce_scatter | solution.py:43
  149.2 0.0 copy-done.8
  149.2 1.7 fusion.13
  150.9 0.0 all-gather.7.cloned.1.call-update
  151.0 0.0 all-gather.9.cloned.1.call-start
  151.0 0.5 all-gather.9.cloned.1.call-update
  151.5 0.0 all-gather.11.cloned.1.call-start
  151.6 0.5 all-gather.11.cloned.1.call-update
  152.1 0.0 reduce-scatter.5.cloned.1.call-start
  152.2 69.8 %all-gather.7.cloned.1.call-done = bf16[2048,384]{1,0:T(8,128)(2,1)} async-done(((bf16[128,384]{1,0:T(8,128)(2,1)}), bf16[2048,384]{1,0:T(8,128)(2,1)}) %all-gather.7.cloned.1.call-update) | async-done | bytes 1572880 | tf_op jit(solution)/shard_map/all_gather | solution.py:54
  222.0 0.0 copy-done.2
  222.0 3.7 convolution_convert_fusion
  225.7 0.0 reduce-scatter.5.cloned.1.call-update
  225.7 0.0 copy-start.6
  225.8 0.0 copy-start.7
  225.8 0.9 copy.16
  226.7 0.0 copy-done.3
  226.7 0.2 copy.19
  226.9 0.0 copy-done.4
  226.9 0.9 copy.18
  227.8 0.0 copy-done.5
  227.8 0.9 copy.17
  228.7 0.0 copy-done.6
  228.7 0.2 copy.22
  228.9 0.0 copy-done.7
  228.9 0.2 copy.20
  229.2 51.6 %all-gather.9.cloned.1.call-done = bf16[2048,384]{1,0:T(8,128)(2,1)} async-done(((bf16[64,384]{1,0:T(8,128)(2,1)}), bf16[2048,384]{1,0:T(8,128)(2,1)}) %all-gather.9.cloned.1.call-update) | async-done | bytes 1572880 | tf_op jit(solution)/shard_map/all_gather | solution.py:56
  280.7 0.0 copy-done.1
  280.7 3.7 fusion.5
  284.5 2.0 copy.25
  286.4 0.9 copy.26
  287.3 0.9 copy.27
  288.2 66.7 %all-gather.11.cloned.1.call-done = bf16[2048,384]{1,0:T(8,128)(2,1)} async-done(((bf16[128,384]{1,0:T(8,128)(2,1)}), bf16[2048,384]{1,0:T(8,128)(2,1)}) %all-gather.11.cloned.1.call-update) | async-done | bytes 1572880 | tf_op jit(solution)/shard_map/all_gather | solution.py:53
  354.9 0.0 copy-done
  354.9 2.8 fusion.4
  357.8 0.9 copy.28
  358.7 0.9 copy.29
  359.5 0.9 copy.30
  360.4 98.0 %reduce-scatter.5.cloned.1.call-done = bf16[64,384]{1,0:T(8,128)(2,1)} async-done(((bf16[2048,384]{1,0:T(8,128)(2,1)}), bf16[64,384]{1,0:T(8,128)(2,1)}) %reduce-scatter.5.cloned.1.call-update) | async-done | bytes 49168 | tf_op jit(solution)/shard_map/reduce_scatter | solution.py:64
  (5 shorter events, 0.0 us)
Async XLA Ops:
  7.2 66.6 %all-gather.5.cloned.1.call-start = ((), (), s32[]{:S(2)}) async-start(), calls=%async_computation.2 | async-start | bytes 1622016 | tf_op jit(solution)/shard_map/all_gather | solution.py:41
  7.9 141.3 %reduce-scatter.3.cloned.1.call-start = ((), (), s32[]{:S(2)}) async-start(), calls=%async_computation.3 | async-start | bytes 1671168 | tf_op jit(solution)/shard_map/reduce_scatter | solution.py:43
  77.5 71.7 %copy-start.8 = (bf16[128,384]{1,0:T(8,128)(2,1)S(1)}, bf16[128,384]{1,0:T(8,128)(2,1)}, u32[]{:S(2)}) copy-start(bf16[128,384]{1,0:T(8,128)(2,1)} %param.11) | copy-start | bytes 294916
  77.5 144.5 %copy-start.2 = (bf16[384,384]{1,0:T(8,128)(2,1)S(1)}, bf16[384,384]{1,0:T(8,128)(2,1)}, u32[]{:S(2)}) copy-start(bf16[384,384]{1,0:T(8,128)(2,1)} %param.12) | copy-start | bytes 884740
  77.5 144.5 %all-gather.7.cloned.1.call-start = ((), (), s32[]{:S(2)}) async-start(), calls=%async_computation.4 | async-start | bytes 1671168 | tf_op jit(solution)/shard_map/all_gather | solution.py:54
  151.0 129.8 %all-gather.9.cloned.1.call-start = ((), (), s32[]{:S(2)}) async-start(), calls=%async_computation.6 | async-start | bytes 1622016 | tf_op jit(solution)/shard_map/all_gather | solution.py:56
  151.5 203.4 %all-gather.11.cloned.1.call-start = ((), (), s32[]{:S(2)}) async-start(), calls=%async_computation.7 | async-start | bytes 1671168 | tf_op jit(solution)/shard_map/all_gather | solution.py:53
  152.1 306.3 %reduce-scatter.5.cloned.1.call-start = ((), (), s32[]{:S(2)}) async-start(), calls=%async_computation.5 | async-start | bytes 1622016 | tf_op jit(solution)/shard_map/reduce_scatter | solution.py:64
  225.7 1.0 copy-start.3
  225.7 1.2 copy-start.4
  225.7 2.1 copy-start.5
  225.7 3.0 copy-start.6
  225.8 3.2 copy-start.7
  226.7 54.1 %copy-start.1 = (bf16[2048,384]{1,0:T(8,128)(2,1)S(1)}, bf16[2048,384]{1,0:T(8,128)(2,1)}, u32[]{:S(2)}) copy-start(bf16[2048,384]{1,0:T(8,128)(2,1)} %all-gather.7.cloned.1.call-done) | copy-start | bytes 4718596
  284.5 70.5 %copy-start = (bf16[2048,384]{1,0:T(8,128)(2,1)S(1)}, bf16[2048,384]{1,0:T(8,128)(2,1)}, u32[]{:S(2)}) copy-start(bf16[2048,384]{1,0:T(8,128)(2,1)} %all-gather.5.cloned.1.call-done) | copy-start | bytes 4718596
Sparse Core Ops, SparseCore 0:
  11.1 62.6 all-gather.4
  77.6 71.5 reduce-scatter.2
  152.1 69.8 all-gather.6
  225.5 55.2 all-gather.8
  282.9 72.0 all-gather.10
  360.4 97.9 reduce-scatter.4
where the time goes:
time: 466 us; the launch traced here: 465 us
  waiting for transfers between devices  425 us (91%)
  between operations  14.2 us (3%)
  matrix products  13.9 us (3%)
  local copies, waits for them, and re-layouts  9.82 us (2%)
    reduce_scatter x1, waiting for transfers between devices, shards(): lax.psum_scatter(lax.dot_general(picked, weight_in, (((1,), (1,)), ((), (...  98 us
    reduce_scatter x1, waiting for transfers between devices, shards(): lax.psum_scatter(lax.dot_general(picked, weight_out, (((1,), (1,)), ((),...  71.7 us
    all_gather x1, waiting for transfers between devices, shards(): lax.all_gather((shared * slopes).astype(jnp.bfloat16), 'col', axis=0, til...  69.8 us
    all_gather x1, waiting for transfers between devices, shards(): lax.all_gather(activated.astype(jnp.bfloat16), 'col', axis=0, tiled=True)  66.7 us
    all_gather x1, waiting for transfers between devices, shards(): rows_grad = lax.all_gather(out_grad, 'row', axis=0, tiled=True)  65.8 us
    all_gather x1, waiting for transfers between devices, shards(): rows_in = lax.all_gather(inputs, 'row', axis=0, tiled=True)  51.6 us
    unnamed x30, local copies, waits for them, and re-layouts  9.82 us
  transfers between devices with their start and end apart: 6, of which 6 were waited for; matrix products, arithmetic and copies ran while one was open for 4% of the time, Pallas kernels for 0%

commit v1 on v0

v1 whole, which is shorter than its diff:
```python
import functools
import math

import jax
import jax.numpy as jnp
from jax import lax
from jax.experimental import pallas as pl
from jax.experimental.pallas import tpu as pltpu
from jax.sharding import PartitionSpec as P

gelu_coef = 0.7978845608
beta_first = 0.9
beta_second = 0.95
learn_rate = 0.003
epsilon_adam = 1e-08
correct_first = 1.0 - 0.9**10
correct_second = 1.0 - 0.95**10

MESH = pl.DeviceIdType.MESH
BF = jnp.bfloat16
F32 = jnp.float32
SUBS = 2


def gelu_parts(preact):
    values = preact.astype(jnp.float32)
    tangent = jnp.tanh(gelu_coef * (values + 0.044715 * values * values * values))
    activated = 0.5 * values * (1.0 + tangent)
    slopes = 0.5 * (1.0 + tangent) + 0.5 * values * (1.0 - tangent * tangent) * gelu_coef * (
        1.0 + 3.0 * 0.044715 * values * values
    )
    return (activated, slopes)


def adam_step(weight, moment, second, grads):
    first_new = beta_first * moment.astype(jnp.float32) + (1.0 - beta_first) * grads
    second_new = beta_second * second.astype(jnp.float32) + (1.0 - beta_second) * grads * grads
    weight_new = weight.astype(jnp.float32) - learn_rate * (first_new / correct_first) / (
        jnp.sqrt(second_new / correct_second) + epsilon_adam
    )
    return (
        weight_new.astype(jnp.bfloat16),
        first_new.astype(jnp.bfloat16),
        second_new.astype(jnp.bfloat16),
    )


def nt_dot(left, right):
    return lax.dot_general(left, right, (((1,), (1,)), ((), ())), preferred_element_type=F32)


def tn_dot(left, right):
    return lax.dot_general(left, right, (((0,), (0,)), ((), ())), preferred_element_type=F32)


class Plan:
    def __init__(self, n_row, n_col, tokens, features, hidden):
        self.nq = n_row // 2
        self.X = math.isqrt(self.nq)
        self.Y = self.nq // self.X
        self.nz = n_col
        self.long = n_col // 2
        self.short = n_col - 1 - self.long
        self.msgs = n_col - 1
        self.TL = tokens
        self.TB = 2 * tokens
        self.DL = features
        self.FL = hidden


def kernel(
    plan,
    og_ref,
    in_ref,
    pre_ref,
    win_ref,
    wout_ref,
    ig_ref,
    gin_ref,
    gout_ref,
    og_all,
    in_all,
    act_all,
    del_all,
    slopes,
    ring,
    sib_out,
    sib_in,
    own,
    rv_a,
    rv_b,
    st_a,
    st_b,
    fin_a,
    fin_b,
    act_s,
    act_r,
    rs_s,
    rs_r,
    del_s,
    del_r,
    og_own_s,
    og_a_s,
    og_b_s,
    og_a_r,
    og_b_r,
    og_sib_s,
    og_sib_r,
    in_own_s,
    in_a_s,
    in_b_s,
    in_a_r,
    in_b_r,
    in_sib_s,
    in_sib_r,
    sib_s,
    sib_r,
    ra_s,
    ra_r,
    rb_s,
    rb_r,
    fa_s,
    fa_r,
    fb_s,
    fb_r,
):
    X, Y, NZ, TL, TB = plan.X, plan.Y, plan.nz, plan.TL, plan.TB
    HALF, MSGS = TL // 2, plan.msgs
    SUB = TB // SUBS
    r = lax.axis_index("row")
    z = lax.axis_index("col")
    q = r // 2
    c = r % 2
    x = q // Y
    y = q % Y
    sgn = 1 - 2 * c
    sib = (r + sgn, z)

    def chip(cx, cy):
        return ((cx * Y + cy) * 2 + c, z)

    def x_peer(j):
        return (x + j) % X

    def y_peer(j):
        return (y + j) % Y

    def remote(src, dst, ssem, rsem, dev):
        return pltpu.make_async_remote_copy(
            src_ref=src, dst_ref=dst, send_sem=ssem, recv_sem=rsem, device_id=dev, device_id_type=MESH
        )

    def rows(buf, start, size):
        return buf.at[pl.ds(pl.multiple_of(start, 16), size)]

    def sign(n):
        return (1 - 2 * (n % 2)) * sgn

    def toward(n):
        return (r, (z + sign(n) + NZ) % NZ)

    def sent_block(n):
        return (z - sign(n) * (n // 2) + 2 * NZ) % NZ

    def got_block(n):
        return (z - sign(n) * (n // 2 + 1) + 2 * NZ) % NZ

    def rs_target(n):
        reach = plan.long - (n % 2) * (plan.long - plan.short)
        return (z + sign(n) * (reach - n // 2) + 2 * NZ) % NZ

    def ring_copy(buf, block, n, sub, ssem, rsem):
        part = rows(buf, block * TB + sub * SUB, SUB)
        return remote(part, part, ssem.at[n, sub], rsem.at[n, sub], toward(n))

    def ring_send(buf, n, ssem, rsem):
        for sub in range(SUBS):
            ring_copy(buf, sent_block(n), n, sub, ssem, rsem).start()

    def ring_pass(buf, n, ssem, rsem):
        for sub in range(SUBS):
            ring_copy(buf, got_block(n), n, sub, ssem, rsem).wait_recv()

            @pl.when(n + 2 < MSGS)
            def _():
                ring_copy(buf, sent_block(n + 2), n + 2, sub, ssem, rsem).start()

    def act_pass(n):
        ring_pass(act_all, n, act_s, act_r)

    def block_rows(buf, cx, cy, part=None, core=None):
        start = ((cx * Y + cy) * 2 + (c if core is None else core)) * TL
        if part is None:
            return rows(buf, start, TL)
        return rows(buf, start + part * HALF, HALF)

    def gather_ops(buf, own_s, a_s, b_s, a_r, b_r, s_s, s_r):
        def whole(j, along_x):
            part = block_rows(buf, x, y)
            if along_x:
                return remote(part, part, own_s.at[0, j - 1], a_r.at[q], chip(x_peer(j), y))
            return remote(part, part, own_s.at[1, j - 1], a_r.at[q], chip(x, y_peer(j)))

        def whole_got(cx, cy):
            part = block_rows(buf, cx, cy)
            return remote(part, part, own_s.at[0, 0], a_r.at[cx * Y + cy], sib)

        def pass_a(j, k):
            cx = x_peer(j)
            part = block_rows(buf, cx, y, 0)
            return remote(part, part, a_s.at[j - 1, k - 1], a_r.at[cx * Y + y], chip(x, y_peer(k)))

        def pass_b(j, k):
            cy = y_peer(j)
            part = block_rows(buf, x, cy, 1)
            return remote(part, part, b_s.at[j - 1, k - 1], b_r.at[x * Y + cy], chip(x_peer(k), y))

        def half_got(cx, cy, part, sem):
            half = block_rows(buf, cx, cy, part)
            return remote(half, half, own_s.at[0, 0], sem.at[cx * Y + cy], sib)

        def to_sib(cx, cy):
            part = block_rows(buf, cx, cy)
            at = cx * Y + cy
            return remote(part, part, s_s.at[at], s_r.at[at], sib)

        def from_sib(cx, cy):
            part = block_rows(buf, cx, cy, core=1 - c)
            at = cx * Y + cy
            return remote(part, part, s_s.at[at], s_r.at[at], sib)

        def first():
            for j in (1, X - 1) + tuple(range(2, X - 1)) if X > 2 else (1,):
                whole(j, True).start()
            for j in (1, Y - 1) + tuple(range(2, Y - 1)) if Y > 2 else (1,):
                whole(j, False).start()
            to_sib(x, y).start()

        def second():
            def step(j, _):
                whole_got(x_peer(j), y).wait_recv()
                for k in range(1, Y):
                    pass_a(j, k).start()
                whole_got(x, y_peer(j)).wait_recv()
                for k in range(1, X):
                    pass_b(j, k).start()
                to_sib(x_peer(j), y).start()
                to_sib(x, y_peer(j)).start()
                return 0

            lax.fori_loop(1, X, step, 0)

        def third():
            def step(i, _):
                cx = x_peer(i // (Y - 1) + 1)
                cy = y_peer(i % (Y - 1) + 1)
                half_got(cx, cy, 0, a_r).wait_recv()
                half_got(cx, cy, 1, b_r).wait_recv()
                to_sib(cx, cy).start()
                return 0

            lax.fori_loop(0, (X - 1) * (Y - 1), step, 0)

        def fourth():
            def step(i, _):
                from_sib(i // Y, i % Y).wait_recv()
                return 0

            lax.fori_loop(0, X * Y, step, 0)

        def sent():
            def step(j, _):
                whole(j, True).wait_send()
                whole(j, False).wait_send()
                for k in range(1, Y):
                    pass_a(j, k).wait_send()
                for k in range(1, X):
                    pass_b(j, k).wait_send()
                return 0

            lax.fori_loop(1, X, step, 0)

            def sib_step(i, _):
                to_sib(i // Y, i % Y).wait_send()
                return 0

            lax.fori_loop(0, X * Y, sib_step, 0)

        return first, second, third, fourth, sent

    og_ops = gather_ops(og_all, og_own_s, og_a_s, og_b_s, og_a_r, og_b_r, og_sib_s, og_sib_r)
    in_ops = gather_ops(in_all, in_own_s, in_a_s, in_b_s, in_a_r, in_b_r, in_sib_s, in_sib_r)

    barrier = pltpu.get_barrier_semaphore()
    friends = [sib, toward(0), toward(1)]
    friends += [chip(x_peer(j), y) for j in range(1, X)]
    friends += [chip(x, y_peer(j)) for j in range(1, Y)]
    for friend in friends:
        pl.semaphore_signal(barrier, inc=1, device_id=friend, device_id_type=MESH)
    mine = pl.ds(pl.multiple_of(r * TL, 16), TL)
    block = pl.ds(pl.multiple_of(z * TB, 16), TB)
    og_all[mine] = og_ref[...]
    in_all[mine] = in_ref[...]
    act, slope = gelu_parts(pre_ref[...])
    act_all[block] = act.astype(BF)
    slopes[...] = slope
    ring[0] = jnp.zeros((TB, plan.FL), BF)
    ring[1] = jnp.zeros((TB, plan.FL), BF)
    gin_ref[...] = jnp.zeros_like(gin_ref)
    gout_ref[...] = jnp.zeros_like(gout_ref)
    pl.semaphore_wait(barrier, len(friends))

    og_ops[0]()
    ring_send(act_all, 0, act_s, act_r)
    ring_send(act_all, 1, act_s, act_r)
    og_ops[1]()
    act_pass(0)
    act_pass(1)
    og_ops[2]()
    act_pass(2)
    act_pass(3)
    og_ops[3]()
    in_ops[0]()

    ACT0 = 4

    def rs_copy(n, sub):
        src = ring.at[n, pl.ds(sub * SUB, SUB)]
        dst = ring.at[n + 2, pl.ds(sub * SUB, SUB)]
        return remote(src, dst, rs_s.at[n, sub], rs_r.at[n, sub], toward(n))

    def rs_step(n, _):
        at = pl.multiple_of(rs_target(n) * TB, 16)
        part = nt_dot(og_all[pl.ds(at, TB)], wout_ref[...]).astype(BF).astype(F32)
        for sub in range(SUBS):
            here = pl.ds(sub * SUB, SUB)

            @pl.when(n >= 2)
            def _():
                rs_copy(n - 2, sub).wait_recv()

            ring[n, here] = (ring[n, here].astype(F32) + part[sub * SUB : (sub + 1) * SUB]).astype(BF)

            @pl.when(n < MSGS)
            def _():
                rs_copy(n, sub).start()

        @pl.when(n + ACT0 < MSGS)
        def _():
            act_pass(n + ACT0)

        @pl.when(n == 3)
        def _():
            in_ops[1]()

        @pl.when(n == 8)
        def _():
            in_ops[2]()

        return 0

    lax.fori_loop(0, NZ, rs_step, 0)
    for sub in range(SUBS):
        rs_copy(MSGS - 1, sub).wait_recv()
    total = ring[NZ - 1].astype(F32) + ring[NZ].astype(F32)
    del_all[block] = (total * slopes[...]).astype(BF)
    ring_send(del_all, 0, del_s, del_r)
    ring_send(del_all, 1, del_s, del_r)
    in_ops[3]()

    def chunk(i):
        sig = (2 * (i % 2) - 1) * sgn
        return (z - sig * ((i + 1) // 2) + 2 * NZ) % NZ

    def sib_copy(t):
        return remote(sib_out.at[t], sib_in.at[t], sib_s.at[t], sib_r.at[t], sib)

    low, high = pl.ds(0, HALF), pl.ds(HALF, HALF)

    def a_copy(t):
        tx, ty = t // Y, t % Y
        return remote(own.at[t, low], rv_a.at[ty, x], ra_s.at[t], ra_r.at[ty, x], chip(tx, y))

    def a_got(ty, sx):
        return remote(rv_a.at[ty, sx], rv_a.at[ty, sx], ra_s.at[0], ra_r.at[ty, sx], sib)

    def b_copy(t):
        tx, ty = t // Y, t % Y
        return remote(own.at[t, high], rv_b.at[tx, y], rb_s.at[t], rb_r.at[tx, y], chip(x, ty))

    def b_got(tx, sy):
        return remote(rv_b.at[tx, sy], rv_b.at[tx, sy], rb_s.at[0], rb_r.at[tx, sy], sib)

    def fa_copy(ty):
        return remote(st_a.at[ty], fin_a.at[y], fa_s.at[ty], fa_r.at[y], chip(x, ty))

    def fb_copy(tx):
        return remote(st_b.at[tx], fin_b.at[x], fb_s.at[tx], fb_r.at[x], chip(tx, y))

    def arrive(i):
        @pl.when(i >= 1)
        def _():
            ring_pass(del_all, i - 1, del_s, del_r)

        t = chunk(i)
        at = pl.multiple_of(t * TB, 16)
        theirs = pl.ds(pl.multiple_of(at + (1 - c) * TL, 16), TL)
        sib_out[t] = nt_dot(del_all[theirs], win_ref[...]).astype(BF)
        sib_copy(t).start()
        ours = pl.ds(pl.multiple_of(at + c * TL, 16), TL)
        own[t] = nt_dot(del_all[ours], win_ref[...]).astype(BF)
        here = pl.ds(at, TB)
        gin_ref[...] += tn_dot(in_all[here], del_all[here])
        gout_ref[...] += tn_dot(act_all[here], og_all[here])

    def pair(i):
        t = chunk(i)
        sib_copy(t).wait_recv()
        own[t] = (own[t].astype(F32) + sib_in[t].astype(F32)).astype(BF)

        @pl.when(t // Y != x)
        def _():
            a_copy(t).start()

        @pl.when(t % Y != y)
        def _():
            b_copy(t).start()

    def line(i):
        t = chunk(i)
        tx, ty = t // Y, t % Y

        @pl.when(tx == x)
        def _():
            total = own[t, low].astype(F32)
            for j in range(1, X):
                a_got(ty, x_peer(j)).wait_recv()
                total = total + rv_a[ty, x_peer(j)].astype(F32)
            st_a[ty] = total.astype(BF)

            @pl.when(ty != y)
            def _():
                fa_copy(ty).start()

        @pl.when(ty == y)
        def _():
            total = own[t, high].astype(F32)
            for j in range(1, Y):
                b_got(tx, y_peer(j)).wait_recv()
                total = total + rv_b[tx, y_peer(j)].astype(F32)
            st_b[tx] = total.astype(BF)

            @pl.when(tx != x)
            def _():
                fb_copy(tx).start()

    LAG1, LAG2 = 2, 4

    def del_step(i, _):
        @pl.when(i < NZ)
        def _():
            arrive(i)

        @pl.when((i >= LAG1) & (i < NZ + LAG1))
        def _():
            pair(i - LAG1)

        @pl.when(i >= LAG2)
        def _():
            line(i - LAG2)

        return 0

    lax.fori_loop(0, NZ + LAG2, del_step, 0)

    total = st_a[y].astype(F32)
    for j in range(1, Y):
        remote(fin_a.at[y_peer(j)], fin_a.at[y_peer(j)], fa_s.at[0], fa_r.at[y_peer(j)], sib).wait_recv()
        total = total + fin_a[y_peer(j)].astype(F32)
    ig_ref[low] = total.astype(BF)
    total = st_b[x].astype(F32)
    for j in range(1, X):
        remote(fin_b.at[x_peer(j)], fin_b.at[x_peer(j)], fb_s.at[0], fb_r.at[x_peer(j)], sib).wait_recv()
        total = total + fin_b[x_peer(j)].astype(F32)
    ig_ref[high] = total.astype(BF)

    og_ops[4]()
    in_ops[4]()

    def ring_sent(n, _):
        for sub in range(SUBS):
            ring_copy(act_all, sent_block(n), n, sub, act_s, act_r).wait_send()
            ring_copy(del_all, sent_block(n), n, sub, del_s, del_r).wait_send()
            rs_copy(n, sub).wait_send()
        return 0

    lax.fori_loop(0, MSGS, ring_sent, 0)

    def sum_sent(t, _):
        sib_copy(t).wait_send()

        @pl.when(t // Y != x)
        def _():
            a_copy(t).wait_send()

        @pl.when(t % Y != y)
        def _():
            b_copy(t).wait_send()

        return 0

    lax.fori_loop(0, X * Y, sum_sent, 0)
    for j in range(1, Y):
        fa_copy(y_peer(j)).wait_send()
    for j in range(1, X):
        fb_copy(x_peer(j)).wait_send()


def exchange(plan, og, inputs, preact, weight_in, weight_out):
    X, Y, NZ, TL, TB, DL, FL = plan.X, plan.Y, plan.nz, plan.TL, plan.TB, plan.DL, plan.FL
    nq, msgs = plan.nq, plan.msgs
    dma = pltpu.SemaphoreType.DMA
    vmem = pl.BlockSpec(memory_space=pltpu.VMEM)
    gather_sems = [
        dma((2, X - 1)),
        dma((X - 1, Y - 1)),
        dma((Y - 1, X - 1)),
        dma((nq,)),
        dma((nq,)),
        dma((nq,)),
        dma((nq,)),
    ]
    return pl.pallas_call(
        functools.partial(kernel, plan),
        out_shape=(
            jax.ShapeDtypeStruct((TL, DL), BF),
            jax.ShapeDtypeStruct((DL, FL), F32),
            jax.ShapeDtypeStruct((FL, DL), F32),
        ),
        in_specs=[vmem] * 5,
        out_specs=(vmem,) * 3,
        scratch_shapes=[
            pltpu.VMEM((nq * TB, DL), BF),
            pltpu.VMEM((nq * TB, DL), BF),
            pltpu.VMEM((NZ * TB, FL), BF),
            pltpu.VMEM((NZ * TB, FL), BF),
            pltpu.VMEM((TB, FL), F32),
            pltpu.VMEM((NZ + 1, TB, FL), BF),
            pltpu.VMEM((NZ, TL, DL), BF),
            pltpu.VMEM((NZ, TL, DL), BF),
            pltpu.VMEM((NZ, TL, DL), BF),
            pltpu.VMEM((Y, X, TL // 2, DL), BF),
            pltpu.VMEM((X, Y, TL // 2, DL), BF),
            pltpu.VMEM((Y, TL // 2, DL), BF),
            pltpu.VMEM((X, TL // 2, DL), BF),
            pltpu.VMEM((Y, TL // 2, DL), BF),
            pltpu.VMEM((X, TL // 2, DL), BF),
        ]
        + [dma((msgs, SUBS))] * 6
        + gather_sems * 2
        + [dma((nq,)), dma((nq,))]
        + [dma((nq,)), dma((Y, X)), dma((nq,)), dma((X, Y))]
        + [dma((Y,)), dma((Y,)), dma((X,)), dma((X,))],
        compiler_params=pltpu.CompilerParams(
            collective_id=0, has_side_effects=True, vmem_limit_bytes=40 * 1024 * 1024
        ),
    )(og, inputs, preact, weight_in, weight_out)


def shards(
    plan, inputs, out_grad, preact, weight_in, weight_out, moment_in, second_in, moment_out, second_out
):
    input_grad, grad_in, grad_out = exchange(plan, out_grad, inputs, preact, weight_in, weight_out)
    weight_a, moment_a, second_a = adam_step(weight_in, moment_in, second_in, grad_in)
    weight_b, moment_b, second_b = adam_step(weight_out, moment_out, second_out, grad_out)
    return (input_grad, weight_a, moment_a, second_a, weight_b, moment_b, second_b)


def solution(mesh):
    n_row, n_col = mesh.shape["row"], mesh.shape["col"]

    def whole(inputs, out_grad, preact, *rest):
        plan = Plan(
            n_row, n_col, inputs.shape[0] // n_row, inputs.shape[1] // n_col, preact.shape[1] // n_row
        )
        by_token, by_weight = P("row", "col"), P("col", "row")
        return jax.shard_map(
            functools.partial(shards, plan),
            mesh=mesh,
            in_specs=(
                by_token,
                by_token,
                by_weight,
                by_weight,
                by_token,
                by_weight,
                by_weight,
                by_token,
                by_token,
            ),
            out_specs=(by_token, by_weight, by_weight, by_weight, by_token, by_token, by_token),
            check_vma=False,
        )(inputs, out_grad, preact, *rest)

    return whole
```

time: 466 us -> 110 us (0.24)
  the two profiles are of different devices: /device:TPU:6 before, /device:TPU:4 now
where the time goes in v1:
time: 110 us
  Pallas kernels  101 us (92%)
  local copies, waits for them, and re-layouts  5.03 us (5%)
  other arithmetic  3.24 us (3%)
    pallas_call x1, Pallas kernels, exchange(): pl.pallas_call(functools.partial(kernel, plan), out_shape=(jax.ShapeDtype...  101 us
    unnamed x15, local copies, waits for them, and re-layouts  5.03 us
    convert_element_type x1, other arithmetic, adam_step(): second_new.astype(jnp.bfloat16)  3.24 us

profile of v1, /device:TPU:4, one launch (start us, length us, event | category | flops | bytes accessed | tf_op | source)
XLA Modules:
  0.0 109.9 jit_solution(4745813086353633339)
XLA Ops:
  0.6 0.0 copy-start
  0.6 1.0 copy-done
  1.6 0.0 copy-start.1
  1.6 1.0 copy-done.1
  2.6 0.0 copy-start.2
  2.6 0.9 copy-done.2
  3.5 0.0 copy-start.3
  3.5 0.8 copy-done.3
  4.3 0.0 copy-start.4
  4.3 0.8 copy-done.4
  5.1 0.0 copy-start.5
  5.1 0.0 copy-start.6
  5.1 101.0 %shard_map.144 = (bf16[64,384]{1,0:T(8,128)(2,1)S(1)}, f32[384,384]{1,0:T(8,128)S(1)}, f32[384,384]{1,0:T(8,128)S(1)}) custom-call(bf16[64,384]{1,0:T(8,128)(2,1)S(1)} %copy-done.3, bf16[64,384]{1,0:T(8,128)(2,1)S(1)} %copy-done.4, bf16[128,384]{1,0:T(8,128)(2,1)S(1)} %copy-done.2, bf16[384,384]{1,0:T(8,128)(2,1)S(1)} %copy-done, bf16[384,384]{1,0:T(8,128)(2,1)S(1)} %copy-done.1), custom_call_target="tpu_custom_call" | custom-call | tf_op jit(solution)/shard_map/pallas_call | solution.py:533
  106.1 0.0 copy-done.5
  106.1 0.0 copy-done.6
  106.1 3.2 %fusion.4 = (bf16[384,384]{1,0:T(8,128)(2,1)}, bf16[384,384]{1,0:T(8,128)(2,1)}, bf16[384,384]{1,0:T(8,128)(2,1)}, bf16[384,384]{1,0:T(8,128)(2,1)}, bf16[384,384]{1,0:T(8,128)(2,1)}, /*index=5*/bf16[384,384]{1,0:T(8,128)(2,1)}) fusion(f32[384,384]{1,0:T(8,128)S(1)} %get-tuple-element.12, bf16[384,384]{1,0:T(8,128)(2,1)S(1)} %copy-done.5, ...), kind=kLoop, calls=%fused_computation.10 | loop fusion | flops 5308416 | bytes 4718592 | tf_op jit(solution)/shard_map/convert_element_type | solution.py:44
  109.3 0.6 copy.17
Async XLA Ops:
  0.6 1.0 copy-start
  1.6 1.0 copy-start.1
  2.6 0.9 copy-start.2
  3.5 0.8 copy-start.3
  4.3 0.8 copy-start.4
  5.1 101.0 %copy-start.5 = (bf16[384,384]{1,0:T(8,128)(2,1)S(1)}, bf16[384,384]{1,0:T(8,128)(2,1)}, u32[]{:S(2)}) copy-start(bf16[384,384]{1,0:T(8,128)(2,1)} %param.17) | copy-start | bytes 884740
  5.1 101.0 %copy-start.6 = (bf16[384,384]{1,0:T(8,128)(2,1)S(1)}, bf16[384,384]{1,0:T(8,128)(2,1)}, u32[]{:S(2)}) copy-start(bf16[384,384]{1,0:T(8,128)(2,1)} %param.16) | copy-start | bytes 884740

commit v2 on v1

v2 whole, which is shorter than its diff:
```python
import functools
import math

import jax
import jax.numpy as jnp
from jax import lax
from jax.experimental import pallas as pl
from jax.experimental.pallas import tpu as pltpu
from jax.sharding import PartitionSpec as P

gelu_coef = 0.7978845608
beta_first = 0.9
beta_second = 0.95
learn_rate = 0.003
epsilon_adam = 1e-08
correct_first = 1.0 - 0.9**10
correct_second = 1.0 - 0.95**10

MESH = pl.DeviceIdType.MESH
BF = jnp.bfloat16
F32 = jnp.float32


def PEERS(n):
    return (1, n - 1) + tuple(range(2, n - 1)) if n > 2 else (1,)


def gelu_parts(preact):
    values = preact.astype(jnp.float32)
    tangent = jnp.tanh(gelu_coef * (values + 0.044715 * values * values * values))
    activated = 0.5 * values * (1.0 + tangent)
    slopes = 0.5 * (1.0 + tangent) + 0.5 * values * (1.0 - tangent * tangent) * gelu_coef * (
        1.0 + 3.0 * 0.044715 * values * values
    )
    return (activated, slopes)


def adam_step(weight, moment, second, grads):
    first_new = beta_first * moment.astype(jnp.float32) + (1.0 - beta_first) * grads
    second_new = beta_second * second.astype(jnp.float32) + (1.0 - beta_second) * grads * grads
    weight_new = weight.astype(jnp.float32) - learn_rate * (first_new / correct_first) / (
        jnp.sqrt(second_new / correct_second) + epsilon_adam
    )
    return (
        weight_new.astype(jnp.bfloat16),
        first_new.astype(jnp.bfloat16),
        second_new.astype(jnp.bfloat16),
    )


def nt_dot(left, right):
    return lax.dot_general(left, right, (((1,), (1,)), ((), ())), preferred_element_type=F32)


def tn_dot(left, right):
    return lax.dot_general(left, right, (((0,), (0,)), ((), ())), preferred_element_type=F32)


class Plan:
    def __init__(self, n_row, n_col, tokens, features, hidden):
        self.nq = n_row // 2
        self.X = math.isqrt(self.nq)
        self.Y = self.nq // self.X
        self.nz = n_col
        self.long = n_col // 2
        self.short = n_col - 1 - self.long
        self.msgs = n_col - 1
        self.TL = tokens
        self.TB = 2 * tokens
        self.DL = features
        self.FL = hidden
        self.subs_act, self.subs_rs, self.subs_del = 2, 4, 4
        self.act_1, self.act_2, self.act_3, self.act_every = 2, 2, 10, 2
        self.lag1, self.lag2 = 3, 7
        self.jump_rs, self.jump_del = 1, 1
        self.call = 0


def kernel(
    plan,
    og_ref,
    in_ref,
    pre_ref,
    win_ref,
    wout_ref,
    ig_ref,
    gin_ref,
    gout_ref,
    og_all,
    in_all,
    act_all,
    del_all,
    pre,
    win,
    wout,
    slopes,
    ring,
    sib_out,
    sib_in,
    own,
    rv_a,
    rv_b,
    st_a,
    st_b,
    fin_a,
    fin_b,
    load,
    sent,
    act_r,
    rs_r,
    del_r,
    og_a_r,
    og_b_r,
    og_sib_r,
    in_a_r,
    in_b_r,
    in_sib_r,
    sib_r,
    ra_r,
    rb_r,
    fa_r,
    fb_r,
):
    X, Y, NZ, TL, TB = plan.X, plan.Y, plan.nz, plan.TL, plan.TB
    HALF, MSGS = TL // 2, plan.msgs
    r = lax.axis_index("row")
    z = lax.axis_index("col")
    q = r // 2
    c = r % 2
    x = q // Y
    y = q % Y
    sgn = 1 - 2 * c
    sib = (r + sgn, z)
    OG, IN, ACT, RS, DEL, SIB, RA, RB, FA, FB = (sent.at[k] for k in range(10))

    def chip(cx, cy):
        return ((cx * Y + cy) * 2 + c, z)

    def x_peer(j):
        return (x + j) % X

    def y_peer(j):
        return (y + j) % Y

    def remote(src, dst, ssem, rsem, dev):
        return pltpu.make_async_remote_copy(
            src_ref=src, dst_ref=dst, send_sem=ssem, recv_sem=rsem, device_id=dev, device_id_type=MESH
        )

    def rows(buf, start, size):
        return buf.at[pl.ds(pl.multiple_of(start, 16), size)]

    def sign(n):
        return (1 - 2 * (n % 2)) * sgn

    def plane(step):
        return (r, (z + step + NZ) % NZ)

    def at_step(i, a):
        return (i + 32 - a) // 32 - (i + 31 - a) // 32

    class Ring:
        def __init__(self, buf, jump, subs, ssem, rsem):
            self.buf, self.jump, self.subs, self.ssem, self.rsem = buf, jump, subs, ssem, rsem

        def copy(self, block, n, sub, hops):
            size = TB // self.subs
            part = rows(self.buf, block * TB + sub * size, size)
            return remote(part, part, self.ssem, self.rsem.at[n, sub], plane(sign(n) * hops))

        def start(self):
            for dist in (1, self.jump) if self.jump > 1 else (1,):
                for n in (2 * dist - 2, 2 * dist - 1):
                    for sub in range(self.subs):
                        self.copy(z, n, sub, dist).start()

        def passed(self, n):
            block = (z - sign(n) * (n // 2 + 1) + 2 * NZ) % NZ
            for sub in range(self.subs):
                self.copy(block, n, sub, 1).wait_recv()

                @pl.when((n + 2 < MSGS) & (n // 2 + 2 != (self.jump if self.jump > 1 else 0)))
                def _():
                    self.copy(block, n + 2, sub, 1).start()

    acts = Ring(act_all, 1, plan.subs_act, ACT, act_r)
    deltas = Ring(del_all, plan.jump_del, plan.subs_del, DEL, del_r)

    def block_rows(buf, cx, cy, part=None, core=None):
        start = ((cx * Y + cy) * 2 + (c if core is None else core)) * TL
        if part is None:
            return rows(buf, start, TL)
        return rows(buf, start + part * HALF, HALF)

    class Gather:
        def __init__(self, buf, ssem, a_r, b_r, s_r):
            self.buf, self.ssem, self.a_r, self.b_r, self.s_r = buf, ssem, a_r, b_r, s_r

        def copy(self, cx, cy, part, sem, dev, core=None):
            ref = block_rows(self.buf, cx, cy, part, core)
            return remote(ref, ref, self.ssem, sem.at[cx * Y + cy], dev)

        def to_sib(self, cx, cy):
            return self.copy(cx, cy, None, self.s_r, sib)

        def from_sib(self, cx, cy):
            return self.copy(cx, cy, None, self.s_r, sib, 1 - c)

        def first(self):
            for j in PEERS(X):
                self.copy(x, y, None, self.a_r, chip(x_peer(j), y)).start()
            for j in PEERS(Y):
                self.copy(x, y, None, self.a_r, chip(x, y_peer(j))).start()
            self.to_sib(x, y).start()

        def second(self, j):
            self.copy(x_peer(j), y, None, self.a_r, sib).wait_recv()
            for k in PEERS(Y):
                self.copy(x_peer(j), y, 0, self.a_r, chip(x, y_peer(k))).start()
            self.copy(x, y_peer(j), None, self.a_r, sib).wait_recv()
            for k in PEERS(X):
                self.copy(x, y_peer(j), 1, self.b_r, chip(x_peer(k), y)).start()
            self.to_sib(x_peer(j), y).start()
            self.to_sib(x, y_peer(j)).start()

        def third(self, i):
            cx = x_peer(i // (Y - 1) + 1)
            cy = y_peer(i % (Y - 1) + 1)
            self.copy(cx, cy, 0, self.a_r, sib).wait_recv()
            self.copy(cx, cy, 1, self.b_r, sib).wait_recv()
            self.to_sib(cx, cy).start()

        def sent(self):
            size = (X + Y - 2) * TL + (X - 1) * (Y - 1) * 2 * HALF + X * Y * TL
            whole = rows(self.buf, 0, size)
            remote(whole, whole, self.ssem, self.s_r.at[0], sib).wait_send()

    THIRDS = (X - 1) * (Y - 1)
    og = Gather(og_all, OG, og_a_r, og_b_r, og_sib_r)
    inp = Gather(in_all, IN, in_a_r, in_b_r, in_sib_r)

    def loop(low, high, body):
        def step(i, _):
            body(i)
            return 0

        lax.fori_loop(low, high, step, 0)

    barrier = pltpu.get_barrier_semaphore()
    friends = [sib]
    for hops in sorted({1, plan.jump_rs, plan.jump_del}):
        friends += [plane(hops), plane(-hops)]
    friends += [chip(x_peer(j), y) for j in range(1, X)]
    friends += [chip(x, y_peer(j)) for j in range(1, Y)]
    for friend in friends:
        pl.semaphore_signal(barrier, inc=1, device_id=friend, device_id_type=MESH)
    get_pre = pltpu.make_async_copy(pre_ref, pre, load.at[0])
    get_og = pltpu.make_async_copy(og_ref, rows(og_all, r * TL, TL), load.at[1])
    get_wout = pltpu.make_async_copy(wout_ref, wout, load.at[2])
    get_in = pltpu.make_async_copy(in_ref, rows(in_all, r * TL, TL), load.at[3])
    get_win = pltpu.make_async_copy(win_ref, win, load.at[4])
    for get in (get_pre, get_og, get_wout, get_in, get_win):
        get.start()
    block = pl.ds(pl.multiple_of(z * TB, 16), TB)
    LONG, SHORT, JUMP = plan.long, plan.short, plan.jump_rs
    FAR, OWN = LONG + 1, LONG + 2
    fresh = [(0, LONG), (1, SHORT), (1, OWN)]
    if JUMP > 1:
        fresh += [(0, JUMP - 1), (1, JUMP - 1)]
    for way, slot in fresh:
        ring[way, slot] = jnp.zeros((TB, plan.FL), BF)
    gin_ref[...] = jnp.zeros_like(gin_ref)
    gout_ref[...] = jnp.zeros_like(gout_ref)
    get_pre.wait()
    act, slope = gelu_parts(pre[...])
    act_all[block] = act.astype(BF)
    slopes[...] = slope
    get_og.wait()
    pl.semaphore_wait(barrier, len(friends))

    og.first()
    acts.start()
    get_in.wait()
    get_wout.wait()
    get_win.wait()
    loop(1, X, og.second)
    loop(0, plan.act_1, acts.passed)
    loop(0, THIRDS, og.third)
    loop(plan.act_1, plan.act_2, acts.passed)
    inp.first()

    def rs_copy(way, dist, sub):
        size = TB // plan.subs_rs
        here = pl.ds(sub * size, size)
        direct = at_step(dist, JUMP)
        into = dist - 1 + direct * (FAR - JUMP + 1)
        hops = 1 + direct * (JUMP - 1)
        return remote(
            ring.at[way, dist, here],
            ring.at[way, into, here],
            RS,
            rs_r.at[way, into, sub],
            plane((1 - 2 * way) * sgn * hops),
        )

    def rs_got(way, slot, sub):
        size = TB // plan.subs_rs
        ref = ring.at[way, slot, pl.ds(sub * size, size)]
        return remote(ref, ref, RS, rs_r.at[way, slot, sub], sib)

    def rs_step(n):
        way = n % 2
        k = n // 2 + way
        dist = LONG - k
        if JUMP > 1:
            dist = dist - at_step(k, LONG - JUMP) + at_step(k, LONG - JUMP + 1)
        t = (z + (1 - 2 * way) * sgn * dist + NZ) % NZ
        og.from_sib(t // Y, t % Y).wait_recv()
        at = pl.multiple_of(t * TB, 16)
        part = nt_dot(og_all[pl.ds(at, TB)], wout[...]).astype(BF).astype(F32)
        size = TB // plan.subs_rs
        slot = dist + at_step(dist, 0) * OWN
        for sub in range(plan.subs_rs):
            here = pl.ds(sub * size, size)

            @pl.when((n >= 2) & (dist != (JUMP - 1 if JUMP > 1 else 0)) & (dist != 0))
            def _():
                rs_got(way, dist, sub).wait_recv()

            ring[way, slot, here] = (
                ring[way, slot, here].astype(F32) + part[sub * size : (sub + 1) * size]
            ).astype(BF)

            @pl.when(dist != 0)
            def _():
                rs_copy(way, dist, sub).start()

        m = plan.act_2 + n // plan.act_every

        @pl.when((n % plan.act_every == plan.act_every - 1) & (m < plan.act_3))
        def _():
            acts.passed(m)

        @pl.when((n >= 2) & (n < 1 + X))
        def _():
            inp.second(n - 1)

        @pl.when((n >= NZ - THIRDS))
        def _():
            inp.third(n - (NZ - THIRDS))

    loop(0, NZ, rs_step)
    total = ring[1, OWN].astype(F32)
    for slot in (0, FAR) if JUMP > 1 else (FAR,):
        for way in (0, 1):
            for sub in range(plan.subs_rs):
                rs_got(way, slot, sub).wait_recv()
            total = total + ring[way, slot].astype(F32)
    del_all[block] = (total * slopes[...]).astype(BF)
    deltas.start()
    loop(0, X * Y, lambda i: inp.from_sib(i // Y, i % Y).wait_recv())

    def far(i):
        k = (i + 1) // 2
        return k + at_step(k, 2) - at_step(k, 3) if plan.jump_del == 3 else k

    def message(i):
        return 2 * far(i) - 1 - i % 2

    def chunk(i):
        sig = (2 * (i % 2) - 1) * sgn
        return (z - sig * far(i) + 2 * NZ) % NZ

    def sib_copy(t):
        return remote(sib_out.at[t], sib_in.at[t], SIB, sib_r.at[t], sib)

    low, high = pl.ds(0, HALF), pl.ds(HALF, HALF)

    def a_copy(t):
        tx, ty = t // Y, t % Y
        return remote(own.at[t, low], rv_a.at[ty, x], RA, ra_r.at[ty, x], chip(tx, y))

    def a_got(ty, sx):
        return remote(rv_a.at[ty, sx], rv_a.at[ty, sx], RA, ra_r.at[ty, sx], sib)

    def b_copy(t):
        tx, ty = t // Y, t % Y
        return remote(own.at[t, high], rv_b.at[tx, y], RB, rb_r.at[tx, y], chip(x, ty))

    def b_got(tx, sy):
        return remote(rv_b.at[tx, sy], rv_b.at[tx, sy], RB, rb_r.at[tx, sy], sib)

    def fa_copy(ty):
        return remote(st_a.at[ty], fin_a.at[y], FA, fa_r.at[y], chip(x, ty))

    def fb_copy(tx):
        return remote(st_b.at[tx], fin_b.at[x], FB, fb_r.at[x], chip(tx, y))

    def arrive(i):
        @pl.when(i >= 1)
        def _():
            deltas.passed(message(i))

        t = chunk(i)
        at = pl.multiple_of(t * TB, 16)
        theirs = pl.ds(pl.multiple_of(at + (1 - c) * TL, 16), TL)
        sib_out[t] = nt_dot(del_all[theirs], win[...]).astype(BF)
        sib_copy(t).start()
        ours = pl.ds(pl.multiple_of(at + c * TL, 16), TL)
        own[t] = nt_dot(del_all[ours], win[...]).astype(BF)

        @pl.when((i >= plan.act_3 + 1) & (i < MSGS + 1))
        def _():
            acts.passed(i - 1)

        here = pl.ds(at, TB)
        gin_ref[...] += tn_dot(in_all[here], del_all[here])
        gout_ref[...] += tn_dot(act_all[here], og_all[here])

    def pair(i):
        t = chunk(i)
        sib_copy(t).wait_recv()
        own[t] = (own[t].astype(F32) + sib_in[t].astype(F32)).astype(BF)

        @pl.when(t // Y != x)
        def _():
            a_copy(t).start()

        @pl.when(t % Y != y)
        def _():
            b_copy(t).start()

    def line(i):
        t = chunk(i)
        tx, ty = t // Y, t % Y

        @pl.when(tx == x)
        def _():
            total = own[t, low].astype(F32)
            for j in range(1, X):
                a_got(ty, x_peer(j)).wait_recv()
                total = total + rv_a[ty, x_peer(j)].astype(F32)
            st_a[ty] = total.astype(BF)

            @pl.when(ty != y)
            def _():
                fa_copy(ty).start()

        @pl.when(ty == y)
        def _():
            total = own[t, high].astype(F32)
            for j in range(1, Y):
                b_got(tx, y_peer(j)).wait_recv()
                total = total + rv_b[tx, y_peer(j)].astype(F32)
            st_b[tx] = total.astype(BF)

            @pl.when(tx != x)
            def _():
                fb_copy(tx).start()

    LAG1, LAG2 = plan.lag1, plan.lag2

    def del_step(i):
        @pl.when(i < NZ)
        def _():
            arrive(i)

        @pl.when((i >= LAG1) & (i < NZ + LAG1))
        def _():
            pair(i - LAG1)

        @pl.when(i >= LAG2)
        def _():
            line(i - LAG2)

    loop(0, NZ + LAG2, del_step)

    og.sent()
    inp.sent()
    messages = rows(act_all, 0, MSGS * TB)
    remote(messages, messages, ACT, act_r.at[0, 0], sib).wait_send()
    remote(messages, messages, DEL, del_r.at[0, 0], sib).wait_send()
    remote(messages, messages, RS, act_r.at[0, 0], sib).wait_send()
    remote(sib_out, sib_out, SIB, sib_r.at[0], sib).wait_send()
    halves = sib_out.at[pl.ds(0, (X - 1) * Y // 2)]
    remote(halves, halves, RA, sib_r.at[0], sib).wait_send()
    halves = sib_out.at[pl.ds(0, (Y - 1) * X // 2)]
    remote(halves, halves, RB, sib_r.at[0], sib).wait_send()

    total = st_a[y].astype(F32)
    for j in range(1, Y):
        remote(fin_a.at[y_peer(j)], fin_a.at[y_peer(j)], FA, fa_r.at[y_peer(j)], sib).wait_recv()
        total = total + fin_a[y_peer(j)].astype(F32)
    ig_ref[low] = total.astype(BF)
    total = st_b[x].astype(F32)
    for j in range(1, X):
        remote(fin_b.at[x_peer(j)], fin_b.at[x_peer(j)], FB, fb_r.at[x_peer(j)], sib).wait_recv()
        total = total + fin_b[x_peer(j)].astype(F32)
    ig_ref[high] = total.astype(BF)
    last = st_a.at[pl.ds(0, Y - 1)]
    remote(last, last, FA, fa_r.at[0], sib).wait_send()
    last = st_b.at[pl.ds(0, X - 1)]
    remote(last, last, FB, fb_r.at[0], sib).wait_send()


def exchange(plan, og, inputs, preact, weight_in, weight_out):
    X, Y, NZ, TL, TB, DL, FL = plan.X, plan.Y, plan.nz, plan.TL, plan.TB, plan.DL, plan.FL
    nq, msgs = plan.nq, plan.msgs
    dma = pltpu.SemaphoreType.DMA
    vmem = pl.BlockSpec(memory_space=pltpu.VMEM)
    hbm = pl.BlockSpec(memory_space=pltpu.HBM)
    return pl.pallas_call(
        functools.partial(kernel, plan),
        out_shape=(
            jax.ShapeDtypeStruct((TL, DL), BF),
            jax.ShapeDtypeStruct((DL, FL), F32),
            jax.ShapeDtypeStruct((FL, DL), F32),
        ),
        in_specs=[hbm] * 5,
        out_specs=(vmem,) * 3,
        scratch_shapes=[
            pltpu.VMEM((nq * TB, DL), BF),
            pltpu.VMEM((nq * TB, DL), BF),
            pltpu.VMEM((NZ * TB, FL), BF),
            pltpu.VMEM((NZ * TB, FL), BF),
            pltpu.VMEM((TB, FL), BF),
            pltpu.VMEM((DL, FL), BF),
            pltpu.VMEM((FL, DL), BF),
            pltpu.VMEM((TB, FL), F32),
            pltpu.VMEM((2, plan.long + 3, TB, FL), BF),
            pltpu.VMEM((NZ, TL, DL), BF),
            pltpu.VMEM((NZ, TL, DL), BF),
            pltpu.VMEM((NZ, TL, DL), BF),
            pltpu.VMEM((Y, X, TL // 2, DL), BF),
            pltpu.VMEM((X, Y, TL // 2, DL), BF),
            pltpu.VMEM((Y, TL // 2, DL), BF),
            pltpu.VMEM((X, TL // 2, DL), BF),
            pltpu.VMEM((Y, TL // 2, DL), BF),
            pltpu.VMEM((X, TL // 2, DL), BF),
            dma((5,)),
            dma((10,)),
            dma((msgs, plan.subs_act)),
            dma((2, plan.long + 2, plan.subs_rs)),
            dma((msgs, plan.subs_del)),
        ]
        + [dma((nq,))] * 7
        + [dma((Y, X)), dma((X, Y)), dma((Y,)), dma((X,))],
        compiler_params=pltpu.CompilerParams(
            collective_id=plan.call, has_side_effects=True, vmem_limit_bytes=40 * 1024 * 1024
        ),
    )(og, inputs, preact, weight_in, weight_out)


def shards(
    plan, inputs, out_grad, preact, weight_in, weight_out, moment_in, second_in, moment_out, second_out
):
    input_grad, grad_in, grad_out = exchange(plan, out_grad, inputs, preact, weight_in, weight_out)
    weight_a, moment_a, second_a = adam_step(weight_in, moment_in, second_in, grad_in)
    weight_b, moment_b, second_b = adam_step(weight_out, moment_out, second_out, grad_out)
    return (input_grad, weight_a, moment_a, second_a, weight_b, moment_b, second_b)


def solution(mesh):
    n_row, n_col = mesh.shape["row"], mesh.shape["col"]

    def whole(inputs, out_grad, preact, *rest):
        plan = Plan(
            n_row, n_col, inputs.shape[0] // n_row, inputs.shape[1] // n_col, preact.shape[1] // n_row
        )
        by_token, by_weight = P("row", "col"), P("col", "row")
        return jax.shard_map(
            functools.partial(shards, plan),
            mesh=mesh,
            in_specs=(
                by_token,
                by_token,
                by_weight,
                by_weight,
                by_token,
                by_weight,
                by_weight,
                by_token,
                by_token,
            ),
            out_specs=(by_token, by_weight, by_weight, by_weight, by_token, by_token, by_token),
            check_vma=False,
        )(inputs, out_grad, preact, *rest)

    return whole
```

time: 110 us -> 104 us (0.945)
  Pallas kernels: 101 us -> 95 us
    pallas_call x1, Pallas kernels: 101 us -> 95 us  [exchange(): pl.pallas_call(functools.partial(kernel, plan), out_shape=(jax.ShapeDtype...]
where the time goes in v2:
time: 104 us
  Pallas kernels  95 us (91%)
  local copies, waits for them, and re-layouts  5.03 us (5%)
  other arithmetic  3.24 us (3%)
    pallas_call x1, Pallas kernels, exchange(): pl.pallas_call(functools.partial(kernel, plan), out_shape=(jax.ShapeDtype...  95 us
    unnamed x15, local copies, waits for them, and re-layouts  5.03 us
    convert_element_type x1, other arithmetic, adam_step(): second_new.astype(jnp.bfloat16)  3.24 us

profile of v2, /device:TPU:4, one launch (start us, length us, event | category | flops | bytes accessed | tf_op | source)
XLA Modules:
  0.0 103.9 jit_solution(7268023341964494259)
XLA Ops:
  0.6 0.0 copy-start
  0.6 1.0 copy-done
  1.6 0.0 copy-start.1
  1.6 1.0 copy-done.1
  2.6 0.0 copy-start.2
  2.6 0.9 copy-done.2
  3.5 0.0 copy-start.3
  3.5 0.8 copy-done.3
  4.3 0.0 copy-start.4
  4.3 0.8 copy-done.4
  5.1 0.0 copy-start.5
  5.1 0.0 copy-start.6
  5.1 95.0 %shard_map.144 = (bf16[64,384]{1,0:T(8,128)(2,1)S(1)}, f32[384,384]{1,0:T(8,128)S(1)}, f32[384,384]{1,0:T(8,128)S(1)}) custom-call(bf16[64,384]{1,0:T(8,128)(2,1)S(1)} %copy-done.3, bf16[64,384]{1,0:T(8,128)(2,1)S(1)} %copy-done.4, bf16[128,384]{1,0:T(8,128)(2,1)S(1)} %copy-done.2, bf16[384,384]{1,0:T(8,128)(2,1)S(1)} %copy-done, bf16[384,384]{1,0:T(8,128)(2,1)S(1)} %copy-done.1), custom_call_target="tpu_custom_call" | custom-call | tf_op jit(solution)/shard_map/pallas_call | solution.py:512
  100.1 0.0 copy-done.5
  100.1 0.0 copy-done.6
  100.1 3.2 %fusion.4 = (bf16[384,384]{1,0:T(8,128)(2,1)}, bf16[384,384]{1,0:T(8,128)(2,1)}, bf16[384,384]{1,0:T(8,128)(2,1)}, bf16[384,384]{1,0:T(8,128)(2,1)}, bf16[384,384]{1,0:T(8,128)(2,1)}, /*index=5*/bf16[384,384]{1,0:T(8,128)(2,1)}) fusion(f32[384,384]{1,0:T(8,128)S(1)} %get-tuple-element.12, bf16[384,384]{1,0:T(8,128)(2,1)S(1)} %copy-done.5, ...), kind=kLoop, calls=%fused_computation.10 | loop fusion | flops 5308416 | bytes 4718592 | tf_op jit(solution)/shard_map/convert_element_type | solution.py:47
  103.3 0.6 copy.17
Async XLA Ops:
  0.6 1.0 copy-start
  1.6 1.0 copy-start.1
  2.6 0.9 copy-start.2
  3.5 0.8 copy-start.3
  4.3 0.8 copy-start.4
  5.1 95.0 %copy-start.5 = (bf16[384,384]{1,0:T(8,128)(2,1)S(1)}, bf16[384,384]{1,0:T(8,128)(2,1)}, u32[]{:S(2)}) copy-start(bf16[384,384]{1,0:T(8,128)(2,1)} %param.17) | copy-start | bytes 884740
  5.1 95.0 %copy-start.6 = (bf16[384,384]{1,0:T(8,128)(2,1)S(1)}, bf16[384,384]{1,0:T(8,128)(2,1)}, u32[]{:S(2)}) copy-start(bf16[384,384]{1,0:T(8,128)(2,1)} %param.16) | copy-start | bytes 884740

commit v3 on v2

--- a/solution.py
+++ b/solution.py
@@ -73,6 +73,8 @@
         self.act_1, self.act_2, self.act_3, self.act_every = 2, 2, 10, 2
         self.lag1, self.lag2 = 3, 7
         self.jump_rs, self.jump_del = 1, 1
+        self.lead, self.in_1 = 4, 2
+        self.ops = 2
         self.call = 0
 
 
@@ -125,10 +127,25 @@
     HALF, MSGS = TL // 2, plan.msgs
     r = lax.axis_index("row")
     z = lax.axis_index("col")
-    q = r // 2
-    c = r % 2
-    x = q // Y
-    y = q % Y
+
+    def div(a, n):
+        if isinstance(a, int):
+            return a // n
+        if plan.ops == 2 and n & (n - 1) == 0:
+            return lax.shift_right_logical(a, jnp.int32(n.bit_length() - 1))
+        return lax.div(a, jnp.int32(n)) if plan.ops else a // n
+
+    def mod(a, n):
+        if isinstance(a, int):
+            return a % n
+        if plan.ops == 2 and n & (n - 1) == 0:
+            return a & (n - 1)
+        return lax.rem(a, jnp.int32(n)) if plan.ops else a % n
+
+    q = div(r, 2)
+    c = mod(r, 2)
+    x = div(q, Y)
+    y = mod(q, Y)
     sgn = 1 - 2 * c
     sib = (r + sgn, z)
     OG, IN, ACT, RS, DEL, SIB, RA, RB, FA, FB = (sent.at[k] for k in range(10))
@@ -137,10 +154,10 @@
         return ((cx * Y + cy) * 2 + c, z)
 
     def x_peer(j):
-        return (x + j) % X
+        return mod(x + j, X)
 
     def y_peer(j):
-        return (y + j) % Y
+        return mod(y + j, Y)
 
     def remote(src, dst, ssem, rsem, dev):
         return pltpu.make_async_remote_copy(
@@ -151,13 +168,13 @@
         return buf.at[pl.ds(pl.multiple_of(start, 16), size)]
 
     def sign(n):
-        return (1 - 2 * (n % 2)) * sgn
+        return (1 - 2 * mod(n, 2)) * sgn
 
     def plane(step):
-        return (r, (z + step + NZ) % NZ)
+        return (r, mod(z + step + NZ, NZ))
 
     def at_step(i, a):
-        return (i + 32 - a) // 32 - (i + 31 - a) // 32
+        return jnp.where(i == a, 1, 0)
 
     class Ring:
         def __init__(self, buf, jump, subs, ssem, rsem):
@@ -175,11 +192,11 @@
                         self.copy(z, n, sub, dist).start()
 
         def passed(self, n):
-            block = (z - sign(n) * (n // 2 + 1) + 2 * NZ) % NZ
+            block = mod(z - sign(n) * (div(n, 2) + 1) + 2 * NZ, NZ)
             for sub in range(self.subs):
                 self.copy(block, n, sub, 1).wait_recv()
 
-                @pl.when((n + 2 < MSGS) & (n // 2 + 2 != (self.jump if self.jump > 1 else 0)))
+                @pl.when((n + 2 < MSGS) & (div(n, 2) + 2 != (self.jump if self.jump > 1 else 0)))
                 def _():
                     self.copy(block, n + 2, sub, 1).start()
 
@@ -213,19 +230,19 @@
                 self.copy(x, y, None, self.a_r, chip(x, y_peer(j))).start()
             self.to_sib(x, y).start()
 
-        def second(self, j):
-            self.copy(x_peer(j), y, None, self.a_r, sib).wait_recv()
+        def second_a(self, cx):
+            self.copy(cx, y, None, self.a_r, sib).wait_recv()
             for k in PEERS(Y):
-                self.copy(x_peer(j), y, 0, self.a_r, chip(x, y_peer(k))).start()
-            self.copy(x, y_peer(j), None, self.a_r, sib).wait_recv()
+                self.copy(cx, y, 0, self.a_r, chip(x, y_peer(k))).start()
+            self.to_sib(cx, y).start()
+
+        def second_b(self, cy):
+            self.copy(x, cy, None, self.a_r, sib).wait_recv()
             for k in PEERS(X):
-                self.copy(x, y_peer(j), 1, self.b_r, chip(x_peer(k), y)).start()
-            self.to_sib(x_peer(j), y).start()
-            self.to_sib(x, y_peer(j)).start()
-
-        def third(self, i):
-            cx = x_peer(i // (Y - 1) + 1)
-            cy = y_peer(i % (Y - 1) + 1)
+                self.copy(x, cy, 1, self.b_r, chip(x_peer(k), y)).start()
+            self.to_sib(x, cy).start()
+
+        def third(self, cx, cy):
             self.copy(cx, cy, 0, self.a_r, sib).wait_recv()
             self.copy(cx, cy, 1, self.b_r, sib).wait_recv()
             self.to_sib(cx, cy).start()
@@ -271,23 +288,52 @@
         ring[way, slot] = jnp.zeros((TB, plan.FL), BF)
     gin_ref[...] = jnp.zeros_like(gin_ref)
     gout_ref[...] = jnp.zeros_like(gout_ref)
+    get_og.wait()
+    pl.semaphore_wait(barrier, len(friends))
+
+    og.first()
     get_pre.wait()
     act, slope = gelu_parts(pre[...])
     act_all[block] = act.astype(BF)
+    acts.start()
     slopes[...] = slope
-    get_og.wait()
-    pl.semaphore_wait(barrier, len(friends))
-
-    og.first()
-    acts.start()
     get_in.wait()
     get_wout.wait()
     get_win.wait()
-    loop(1, X, og.second)
+
+    def needed(n):
+        way = mod(n, 2)
+        k = div(n, 2) + way
+        dist = LONG - k
+        if JUMP > 1:
+            dist = dist - at_step(k, LONG - JUMP) + at_step(k, LONG - JUMP + 1)
+        return way, dist, mod(z + (1 - 2 * way) * sgn * dist + NZ, NZ)
+
+    def og_near(n):
+        t = needed(n)[2]
+        tx, ty = div(t, Y), mod(t, Y)
+
+        @pl.when((tx != x) & (ty == y))
+        def _():
+            og.second_a(tx)
+
+        @pl.when((tx == x) & (ty != y))
+        def _():
+            og.second_b(ty)
+
+    def og_far(n):
+        t = needed(n)[2]
+        tx, ty = div(t, Y), mod(t, Y)
+
+        @pl.when((tx != x) & (ty != y))
+        def _():
+            og.third(tx, ty)
+
+    LEAD = plan.lead
+    loop(0, NZ, og_near)
     loop(0, plan.act_1, acts.passed)
-    loop(0, THIRDS, og.third)
+    loop(0, LEAD, og_far)
     loop(plan.act_1, plan.act_2, acts.passed)
-    inp.first()
 
     def rs_copy(way, dist, sub):
         size = TB // plan.subs_rs
@@ -309,17 +355,17 @@
         return remote(ref, ref, RS, rs_r.at[way, slot, sub], sib)
 
     def rs_step(n):
-        way = n % 2
-        k = n // 2 + way
-        dist = LONG - k
-        if JUMP > 1:
-            dist = dist - at_step(k, LONG - JUMP) + at_step(k, LONG - JUMP + 1)
-        t = (z + (1 - 2 * way) * sgn * dist + NZ) % NZ
-        og.from_sib(t // Y, t % Y).wait_recv()
+        way, dist, t = needed(n)
+
+        @pl.when(n + LEAD < NZ)
+        def _():
+            og_far(n + LEAD)
+
+        og.from_sib(div(t, Y), mod(t, Y)).wait_recv()
         at = pl.multiple_of(t * TB, 16)
         part = nt_dot(og_all[pl.ds(at, TB)], wout[...]).astype(BF).astype(F32)
         size = TB // plan.subs_rs
-        slot = dist + at_step(dist, 0) * OWN
+        slot = jnp.where(dist == 0, OWN, dist)
         for sub in range(plan.subs_rs):
             here = pl.ds(sub * size, size)
 
@@ -335,19 +381,26 @@
             def _():
                 rs_copy(way, dist, sub).start()
 
-        m = plan.act_2 + n // plan.act_every
-
-        @pl.when((n % plan.act_every == plan.act_every - 1) & (m < plan.act_3))
+        m = plan.act_2 + div(n, plan.act_every)
+
+        @pl.when((mod(n, plan.act_every) == plan.act_every - 1) & (m < plan.act_3))
         def _():
             acts.passed(m)
 
-        @pl.when((n >= 2) & (n < 1 + X))
-        def _():
-            inp.second(n - 1)
+        @pl.when(n == plan.in_1)
+        def _():
+            inp.first()
+
+        @pl.when((n > NZ - THIRDS - X) & (n < NZ - THIRDS))
+        def _():
+            j = n - (NZ - THIRDS - X)
+            inp.second_a(x_peer(j))
+            inp.second_b(y_peer(j))
 
         @pl.when((n >= NZ - THIRDS))
         def _():
-            inp.third(n - (NZ - THIRDS))
+            i = n - (NZ - THIRDS)
+            inp.third(x_peer(div(i, Y - 1) + 1), y_peer(mod(i, Y - 1) + 1))
 
     loop(0, NZ, rs_step)
     total = ring[1, OWN].astype(F32)
@@ -358,18 +411,18 @@
             total = total + ring[way, slot].astype(F32)
     del_all[block] = (total * slopes[...]).astype(BF)
     deltas.start()
-    loop(0, X * Y, lambda i: inp.from_sib(i // Y, i % Y).wait_recv())
+    loop(0, X * Y, lambda i: inp.from_sib(div(i, Y), mod(i, Y)).wait_recv())
 
     def far(i):
-        k = (i + 1) // 2
+        k = div(i + 1, 2)
         return k + at_step(k, 2) - at_step(k, 3) if plan.jump_del == 3 else k
 
     def message(i):
-        return 2 * far(i) - 1 - i % 2
+        return 2 * far(i) - 1 - mod(i, 2)
 
     def chunk(i):
-        sig = (2 * (i % 2) - 1) * sgn
-        return (z - sig * far(i) + 2 * NZ) % NZ
+        sig = (2 * mod(i, 2) - 1) * sgn
+        return mod(z - sig * far(i) + 2 * NZ, NZ)
 
     def sib_copy(t):
         return remote(sib_out.at[t], sib_in.at[t], SIB, sib_r.at[t], sib)
@@ -377,14 +430,14 @@
     low, high = pl.ds(0, HALF), pl.ds(HALF, HALF)
 
     def a_copy(t):
-        tx, ty = t // Y, t % Y
+        tx, ty = div(t, Y), mod(t, Y)
         return remote(own.at[t, low], rv_a.at[ty, x], RA, ra_r.at[ty, x], chip(tx, y))
 
     def a_got(ty, sx):
         return remote(rv_a.at[ty, sx], rv_a.at[ty, sx], RA, ra_r.at[ty, sx], sib)
 
     def b_copy(t):
-        tx, ty = t // Y, t % Y
+        tx, ty = div(t, Y), mod(t, Y)
         return remote(own.at[t, high], rv_b.at[tx, y], RB, rb_r.at[tx, y], chip(x, ty))
 
     def b_got(tx, sy):
@@ -422,17 +475,17 @@
         sib_copy(t).wait_recv()
         own[t] = (own[t].astype(F32) + sib_in[t].astype(F32)).astype(BF)
 
-        @pl.when(t // Y != x)
+        @pl.when(div(t, Y) != x)
         def _():
             a_copy(t).start()
 
-        @pl.when(t % Y != y)
+        @pl.when(mod(t, Y) != y)
         def _():
             b_copy(t).start()
 
     def line(i):
         t = chunk(i)
-        tx, ty = t // Y, t % Y
+        tx, ty = div(t, Y), mod(t, Y)
 
         @pl.when(tx == x)
         def _():
@@ -546,7 +599,7 @@
         + [dma((nq,))] * 7
         + [dma((Y, X)), dma((X, Y)), dma((Y,)), dma((X,))],
         compiler_params=pltpu.CompilerParams(
-            collective_id=plan.call, has_side_effects=True, vmem_limit_bytes=40 * 1024 * 1024
+            collective_id=plan.call, has_side_effects=True, vmem_limit_bytes=60 * 1024 * 1024
         ),
     )(og, inputs, preact, weight_in, weight_out)
 

time: 104 us -> 99.9 us (0.961)
  local copies, waits for them, and re-layouts: 5.03 us -> 0.63 us
    unnamed x15 -> x7, local copies, waits for them, and re-layouts: 5.03 us -> 0.63 us
where the time goes in v3:
time: 99.9 us; the launch traced here: 99.7 us
  Pallas kernels  94.6 us (95%)
  other arithmetic  3.78 us (4%)
    pallas_call x1, Pallas kernels, exchange(): pl.pallas_call(functools.partial(kernel, plan), out_shape=(jax.ShapeDtype...  94.6 us
    convert_element_type x1, other arithmetic, adam_step(): second_new.astype(jnp.bfloat16)  3.78 us

profile of v3, /device:TPU:4, one launch (start us, length us, event | category | flops | bytes accessed | tf_op | source)
XLA Modules:
  0.0 99.7 jit_solution(5387761443492985929)
XLA Ops:
  0.6 0.0 copy-start.1
  0.6 0.0 copy-start
  0.7 94.6 %shard_map.144 = (bf16[64,384]{1,0:T(8,128)(2,1)}, f32[384,384]{1,0:T(8,128)}, f32[384,384]{1,0:T(8,128)}) custom-call(bf16[64,384]{1,0:T(8,128)(2,1)} %og_ref.1, bf16[64,384]{1,0:T(8,128)(2,1)} %in_ref.1, bf16[128,384]{1,0:T(8,128)(2,1)} %pre_ref.1, bf16[384,384]{1,0:T(8,128)(2,1)} %win_ref.1, bf16[384,384]{1,0:T(8,128)(2,1)} %wout_ref.1), custom_call_target="tpu_custom_call" | custom-call | tf_op jit(solution)/shard_map/pallas_call | solution.py:565
  95.3 0.0 copy-done.1
  95.3 0.0 copy-done
  95.3 0.0 copy-start.2
  95.3 3.8 %fusion.4 = (bf16[384,384]{1,0:T(8,128)(2,1)}, bf16[384,384]{1,0:T(8,128)(2,1)}, bf16[384,384]{1,0:T(8,128)(2,1)}, bf16[384,384]{1,0:T(8,128)(2,1)}, bf16[384,384]{1,0:T(8,128)(2,1)}, /*index=5*/bf16[384,384]{1,0:T(8,128)(2,1)}) fusion(f32[384,384]{1,0:T(8,128)} %get-tuple-element.12, bf16[384,384]{1,0:T(8,128)(2,1)} %param.17, bf16[384,384]{1,0:T(8,128)(2,1)} %param.16, ...), kind=kLoop, calls=%fused_computation.10 | loop fusion | flops 5308416 | bytes 4718592 | tf_op jit(solution)/shard_map/convert_element_type | solution.py:47
  99.1 0.0 copy-done.2
  99.1 0.6 copy.17
Async XLA Ops:
  0.6 94.6 %copy-start.1 = (bf16[384,384]{1,0:T(8,128)(2,1)S(1)}, bf16[384,384]{1,0:T(8,128)(2,1)}, u32[]{:S(2)}) copy-start(bf16[384,384]{1,0:T(8,128)(2,1)} %wout_ref.1) | copy-start | bytes 884740
  0.6 94.6 %copy-start = (bf16[384,384]{1,0:T(8,128)(2,1)S(1)}, bf16[384,384]{1,0:T(8,128)(2,1)}, u32[]{:S(2)}) copy-start(bf16[384,384]{1,0:T(8,128)(2,1)} %win_ref.1) | copy-start | bytes 884740
  95.3 3.8 %copy-start.2 = (bf16[64,384]{1,0:T(8,128)(2,1)S(1)}, bf16[64,384]{1,0:T(8,128)(2,1)}, u32[]{:S(2)}) copy-start(bf16[64,384]{1,0:T(8,128)(2,1)} %get-tuple-element.29) | copy-start | bytes 147460

commit v4 on v3

--- a/solution.py
+++ b/solution.py
@@ -73,7 +73,8 @@
         self.act_1, self.act_2, self.act_3, self.act_every = 2, 2, 10, 2
         self.lag1, self.lag2 = 3, 7
         self.jump_rs, self.jump_del = 1, 1
-        self.lead, self.in_1 = 4, 2
+        self.lead, self.in_1, self.early, self.act_4 = 4, 2, 5, 11
+        self.adam_rows = 32
         self.ops = 2
         self.call = 0
 
@@ -85,9 +86,17 @@
     pre_ref,
     win_ref,
     wout_ref,
+    moment_in_ref,
+    second_in_ref,
+    moment_out_ref,
+    second_out_ref,
     ig_ref,
-    gin_ref,
-    gout_ref,
+    new_win_ref,
+    new_moment_in_ref,
+    new_second_in_ref,
+    new_wout_ref,
+    new_moment_out_ref,
+    new_second_out_ref,
     og_all,
     in_all,
     act_all,
@@ -95,6 +104,12 @@
     pre,
     win,
     wout,
+    moments_in,
+    seconds_in,
+    moments_out,
+    seconds_out,
+    gin_ref,
+    gout_ref,
     slopes,
     ring,
     sib_out,
@@ -276,7 +291,18 @@
     get_wout = pltpu.make_async_copy(wout_ref, wout, load.at[2])
     get_in = pltpu.make_async_copy(in_ref, rows(in_all, r * TL, TL), load.at[3])
     get_win = pltpu.make_async_copy(win_ref, win, load.at[4])
-    for get in (get_pre, get_og, get_wout, get_in, get_win):
+    get_adam = [
+        pltpu.make_async_copy(ref, buf, load.at[5 + k])
+        for k, (ref, buf) in enumerate(
+            (
+                (moment_out_ref, moments_out),
+                (second_out_ref, seconds_out),
+                (moment_in_ref, moments_in),
+                (second_in_ref, seconds_in),
+            )
+        )
+    ]
+    for get in [get_og, get_pre, get_wout, get_in, get_win] + get_adam:
         get.start()
     block = pl.ds(pl.multiple_of(z * TB, 16), TB)
     LONG, SHORT, JUMP = plan.long, plan.short, plan.jump_rs
@@ -291,11 +317,21 @@
     get_og.wait()
     pl.semaphore_wait(barrier, len(friends))
 
-    og.first()
+    late = jnp.minimum(mod(q - z + NZ, NZ), mod(z - q + NZ, NZ)) < plan.early
+
+    @pl.when(jnp.logical_not(late))
+    def _():
+        og.first()
+
     get_pre.wait()
     act, slope = gelu_parts(pre[...])
     act_all[block] = act.astype(BF)
     acts.start()
+
+    @pl.when(late)
+    def _():
+        og.first()
+
     slopes[...] = slope
     get_in.wait()
     get_wout.wait()
@@ -420,9 +456,12 @@
     def message(i):
         return 2 * far(i) - 1 - mod(i, 2)
 
+    def token_block(i, hops):
+        sig = (2 * mod(i, 2) - 1) * sgn
+        return mod(z - sig * hops + 2 * NZ, NZ)
+
     def chunk(i):
-        sig = (2 * mod(i, 2) - 1) * sgn
-        return mod(z - sig * far(i) + 2 * NZ, NZ)
+        return token_block(i, far(i))
 
     def sib_copy(t):
         return remote(sib_out.at[t], sib_in.at[t], SIB, sib_r.at[t], sib)
@@ -456,18 +495,16 @@
 
         t = chunk(i)
         at = pl.multiple_of(t * TB, 16)
-        theirs = pl.ds(pl.multiple_of(at + (1 - c) * TL, 16), TL)
-        sib_out[t] = nt_dot(del_all[theirs], win[...]).astype(BF)
+        here = pl.ds(at, TB)
+        both = nt_dot(del_all[here], win[...]).astype(BF)
+        halves = (both[:TL], both[TL:])
+        sib_out[t] = jnp.where(c == 0, halves[1], halves[0])
         sib_copy(t).start()
-        ours = pl.ds(pl.multiple_of(at + c * TL, 16), TL)
-        own[t] = nt_dot(del_all[ours], win[...]).astype(BF)
-
-        @pl.when((i >= plan.act_3 + 1) & (i < MSGS + 1))
-        def _():
-            acts.passed(i - 1)
-
-        here = pl.ds(at, TB)
+        own[t] = jnp.where(c == 0, halves[0], halves[1])
         gin_ref[...] += tn_dot(in_all[here], del_all[here])
+
+    def add_out(i):
+        here = pl.ds(pl.multiple_of(token_block(i, div(i + 1, 2)) * TB, 16), TB)
         gout_ref[...] += tn_dot(act_all[here], og_all[here])
 
     def pair(i):
@@ -511,14 +548,44 @@
             def _():
                 fb_copy(tx).start()
 
+    ROWS = plan.adam_rows
+
+    def adam(weight, moment, second, grads, low, high):
+        def some(k):
+            here = pl.ds(pl.multiple_of(k * ROWS, ROWS), ROWS)
+            new = adam_step(weight[here], moment[here], second[here], grads[here])
+            weight[here], moment[here], second[here] = new
+
+        loop(low, high, some)
+
+    put_out = [
+        pltpu.make_async_copy(buf, ref, load.at[9 + k])
+        for k, (ref, buf) in enumerate(
+            ((new_wout_ref, wout), (new_moment_out_ref, moments_out), (new_second_out_ref, seconds_out))
+        )
+    ]
+    put_in = [
+        pltpu.make_async_copy(buf, ref, load.at[12 + k])
+        for k, (ref, buf) in enumerate(
+            ((new_win_ref, win), (new_moment_in_ref, moments_in), (new_second_in_ref, seconds_in))
+        )
+    ]
+
     LAG1, LAG2 = plan.lag1, plan.lag2
 
     def del_step(i):
-        @pl.when(i < NZ)
-        def _():
-            arrive(i)
-
-        @pl.when((i >= LAG1) & (i < NZ + LAG1))
+        arrive(i)
+
+        @pl.when(i <= plan.act_3)
+        def _():
+            add_out(i)
+
+        @pl.when((i >= plan.act_4) & (i < plan.act_4 + MSGS - plan.act_3))
+        def _():
+            acts.passed(plan.act_3 + i - plan.act_4)
+            add_out(plan.act_3 + i - plan.act_4 + 1)
+
+        @pl.when(i >= LAG1)
         def _():
             pair(i - LAG1)
 
@@ -526,7 +593,23 @@
         def _():
             line(i - LAG2)
 
-    loop(0, NZ + LAG2, del_step)
+    loop(0, NZ, del_step)
+    for get in get_adam:
+        get.wait()
+    loop(NZ - LAG1, NZ - 1, pair)
+    blocks = plan.FL // ROWS
+    adam(wout, moments_out, seconds_out, gout_ref, 0, blocks // 2)
+    pair(NZ - 1)
+    loop(NZ - LAG2, NZ - 1, line)
+    adam(wout, moments_out, seconds_out, gout_ref, blocks // 2, blocks)
+    for put in put_out:
+        put.start()
+    blocks = plan.DL // ROWS
+    adam(win, moments_in, seconds_in, gin_ref, 0, blocks // 2)
+    line(NZ - 1)
+    adam(win, moments_in, seconds_in, gin_ref, blocks // 2, blocks)
+    for put in put_in:
+        put.start()
 
     og.sent()
     inp.sent()
@@ -550,13 +633,15 @@
         remote(fin_b.at[x_peer(j)], fin_b.at[x_peer(j)], FB, fb_r.at[x_peer(j)], sib).wait_recv()
         total = total + fin_b[x_peer(j)].astype(F32)
     ig_ref[high] = total.astype(BF)
+    for put in put_out + put_in:
+        put.wait()
     last = st_a.at[pl.ds(0, Y - 1)]
     remote(last, last, FA, fa_r.at[0], sib).wait_send()
     last = st_b.at[pl.ds(0, X - 1)]
     remote(last, last, FB, fb_r.at[0], sib).wait_send()
 
 
-def exchange(plan, og, inputs, preact, weight_in, weight_out):
+def exchange(plan, *operands):
     X, Y, NZ, TL, TB, DL, FL = plan.X, plan.Y, plan.nz, plan.TL, plan.TB, plan.DL, plan.FL
     nq, msgs = plan.nq, plan.msgs
     dma = pltpu.SemaphoreType.DMA
@@ -564,13 +649,11 @@
     hbm = pl.BlockSpec(memory_space=pltpu.HBM)
     return pl.pallas_call(
         functools.partial(kernel, plan),
-        out_shape=(
-            jax.ShapeDtypeStruct((TL, DL), BF),
-            jax.ShapeDtypeStruct((DL, FL), F32),
-            jax.ShapeDtypeStruct((FL, DL), F32),
-        ),
-        in_specs=[hbm] * 5,
-        out_specs=(vmem,) * 3,
+        out_shape=(jax.ShapeDtypeStruct((TL, DL), BF),)
+        + (jax.ShapeDtypeStruct((DL, FL), BF),) * 3
+        + (jax.ShapeDtypeStruct((FL, DL), BF),) * 3,
+        in_specs=[hbm] * 9,
+        out_specs=(vmem,) + (hbm,) * 6,
         scratch_shapes=[
             pltpu.VMEM((nq * TB, DL), BF),
             pltpu.VMEM((nq * TB, DL), BF),
@@ -579,6 +662,12 @@
             pltpu.VMEM((TB, FL), BF),
             pltpu.VMEM((DL, FL), BF),
             pltpu.VMEM((FL, DL), BF),
+            pltpu.VMEM((DL, FL), BF),
+            pltpu.VMEM((DL, FL), BF),
+            pltpu.VMEM((FL, DL), BF),
+            pltpu.VMEM((FL, DL), BF),
+            pltpu.VMEM((DL, FL), F32),
+            pltpu.VMEM((FL, DL), F32),
             pltpu.VMEM((TB, FL), F32),
             pltpu.VMEM((2, plan.long + 3, TB, FL), BF),
             pltpu.VMEM((NZ, TL, DL), BF),
@@ -590,7 +679,7 @@
             pltpu.VMEM((X, TL // 2, DL), BF),
             pltpu.VMEM((Y, TL // 2, DL), BF),
             pltpu.VMEM((X, TL // 2, DL), BF),
-            dma((5,)),
+            dma((15,)),
             dma((10,)),
             dma((msgs, plan.subs_act)),
             dma((2, plan.long + 2, plan.subs_rs)),
@@ -601,16 +690,47 @@
         compiler_params=pltpu.CompilerParams(
             collective_id=plan.call, has_side_effects=True, vmem_limit_bytes=60 * 1024 * 1024
         ),
-    )(og, inputs, preact, weight_in, weight_out)
+    )(*operands)
+
+
+def hand_over(*refs):
+    n = len(refs) // 2
+    copies = [pltpu.make_async_copy(refs[k], refs[n + k], refs[-1].at[k]) for k in range(n)]
+    for copy in copies:
+        copy.start()
+    for copy in copies:
+        copy.wait()
+
+
+def results(*arrays):
+    hbm = pl.BlockSpec(memory_space=pltpu.HBM)
+    return pl.pallas_call(
+        hand_over,
+        out_shape=tuple(jax.ShapeDtypeStruct(a.shape, a.dtype) for a in arrays),
+        in_specs=[hbm] * len(arrays),
+        out_specs=(hbm,) * len(arrays),
+        scratch_shapes=[pltpu.SemaphoreType.DMA((len(arrays),))],
+        compiler_params=pltpu.CompilerParams(vmem_limit_bytes=60 * 1024 * 1024),
+    )(*arrays)
 
 
 def shards(
     plan, inputs, out_grad, preact, weight_in, weight_out, moment_in, second_in, moment_out, second_out
 ):
-    input_grad, grad_in, grad_out = exchange(plan, out_grad, inputs, preact, weight_in, weight_out)
-    weight_a, moment_a, second_a = adam_step(weight_in, moment_in, second_in, grad_in)
-    weight_b, moment_b, second_b = adam_step(weight_out, moment_out, second_out, grad_out)
-    return (input_grad, weight_a, moment_a, second_a, weight_b, moment_b, second_b)
+    return results(
+        *exchange(
+            plan,
+            out_grad,
+            inputs,
+            preact,
+            weight_in,
+            weight_out,
+            moment_in,
+            second_in,
+            moment_out,
+            second_out,
+        )
+    )
 
 
 def solution(mesh):

time: 99.9 us -> 151 us (1.51)
  Pallas kernels: 94.6 us -> 150 us
  other arithmetic: 3.78 us -> 0 us
    pallas_call x0 -> x1, Pallas kernels: none -> 56.3 us  [results(): pl.pallas_call(hand_over, out_shape=tuple((jax.ShapeDtypeStruct(a.shape,...]
    convert_element_type x1 -> x0, other arithmetic: 3.78 us -> none  [adam_step(): second_new.astype(jnp.bfloat16)]
where the time goes in v4:
time: 151 us
  Pallas kernels  150 us (99%)
    pallas_call x1, Pallas kernels, exchange(): pl.pallas_call(functools.partial(kernel, plan), out_shape=(jax.ShapeDtype...  94.2 us
    pallas_call x1, Pallas kernels, results(): pl.pallas_call(hand_over, out_shape=tuple((jax.ShapeDtypeStruct(a.shape,...  56.3 us

profile of v4, /device:TPU:4, one launch (start us, length us, event | category | flops | bytes accessed | tf_op | source)
XLA Modules:
  0.0 151.1 jit_solution(7217083057733772983)
XLA Ops:
  0.6 94.2 %shard_map.144 = (bf16[64,384]{1,0:T(8,128)(2,1)}, bf16[384,384]{1,0:T(8,128)(2,1)}, bf16[384,384]{1,0:T(8,128)(2,1)}, bf16[384,384]{1,0:T(8,128)(2,1)}, bf16[38...) custom-call(bf16[64,384]{1,0:T(8,128)(2,1)} %og_ref.1, bf16[64,384]{1,0:T(8,128)(2,1)} %in_ref.1, ...), custom_call_target="tpu_custom_call" | custom-call | tf_op jit(solution)/shard_map/pallas_call | solution.py:650
  94.9 56.3 %shard_map.145 = (bf16[64,384]{1,0:T(8,128)(2,1)}, bf16[384,384]{1,0:T(8,128)(2,1)}, bf16[384,384]{1,0:T(8,128)(2,1)}, bf16[384,384]{1,0:T(8,128)(2,1)}, bf16[38...) custom-call(bf16[64,384]{1,0:T(8,128)(2,1)} %get-tuple-element.14.refs_0_, ...), custom_call_target="tpu_custom_call" | custom-call | tf_op jit(solution)/shard_map/pallas_call | solution.py:707

commit v5 on v4

--- a/solution.py
+++ b/solution.py
@@ -225,8 +225,8 @@
         return rows(buf, start + part * HALF, HALF)
 
     class Gather:
-        def __init__(self, buf, ssem, a_r, b_r, s_r):
-            self.buf, self.ssem, self.a_r, self.b_r, self.s_r = buf, ssem, a_r, b_r, s_r
+        def __init__(self, source, buf, ssem, a_r, b_r, s_r):
+            self.source, self.buf, self.ssem, self.a_r, self.b_r, self.s_r = source, buf, ssem, a_r, b_r, s_r
 
         def copy(self, cx, cy, part, sem, dev, core=None):
             ref = block_rows(self.buf, cx, cy, part, core)
@@ -239,11 +239,12 @@
             return self.copy(cx, cy, None, self.s_r, sib, 1 - c)
 
         def first(self):
+            ref = block_rows(self.buf, x, y)
             for j in PEERS(X):
-                self.copy(x, y, None, self.a_r, chip(x_peer(j), y)).start()
+                remote(self.source, ref, self.ssem, self.a_r.at[q], chip(x_peer(j), y)).start()
             for j in PEERS(Y):
-                self.copy(x, y, None, self.a_r, chip(x, y_peer(j))).start()
-            self.to_sib(x, y).start()
+                remote(self.source, ref, self.ssem, self.a_r.at[q], chip(x, y_peer(j))).start()
+            remote(self.source, ref, self.ssem, self.s_r.at[q], sib).start()
 
         def second_a(self, cx):
             self.copy(cx, y, None, self.a_r, sib).wait_recv()
@@ -268,8 +269,8 @@
             remote(whole, whole, self.ssem, self.s_r.at[0], sib).wait_send()
 
     THIRDS = (X - 1) * (Y - 1)
-    og = Gather(og_all, OG, og_a_r, og_b_r, og_sib_r)
-    inp = Gather(in_all, IN, in_a_r, in_b_r, in_sib_r)
+    og = Gather(og_ref, og_all, OG, og_a_r, og_b_r, og_sib_r)
+    inp = Gather(in_ref, in_all, IN, in_a_r, in_b_r, in_sib_r)
 
     def loop(low, high, body):
         def step(i, _):
@@ -314,7 +315,6 @@
         ring[way, slot] = jnp.zeros((TB, plan.FL), BF)
     gin_ref[...] = jnp.zeros_like(gin_ref)
     gout_ref[...] = jnp.zeros_like(gout_ref)
-    get_og.wait()
     pl.semaphore_wait(barrier, len(friends))
 
     late = jnp.minimum(mod(q - z + NZ, NZ), mod(z - q + NZ, NZ)) < plan.early
@@ -333,6 +333,7 @@
         og.first()
 
     slopes[...] = slope
+    get_og.wait()
     get_in.wait()
     get_wout.wait()
     get_win.wait()
@@ -694,22 +695,28 @@
 
 
 def hand_over(*refs):
-    n = len(refs) // 2
-    copies = [pltpu.make_async_copy(refs[k], refs[n + k], refs[-1].at[k]) for k in range(n)]
-    for copy in copies:
-        copy.start()
-    for copy in copies:
-        copy.wait()
+    n = (len(refs) - 2) // 3
+    sources, targets, held, (came, left) = refs[:n], refs[n : 2 * n], refs[2 * n : 3 * n], refs[3 * n :]
+    loads = [pltpu.make_async_copy(sources[k], held[k], came.at[k]) for k in range(n)]
+    stores = [pltpu.make_async_copy(held[k], targets[k], left.at[k]) for k in range(n)]
+    for load in loads:
+        load.start()
+    for load, store in zip(loads, stores):
+        load.wait()
+        store.start()
+    for store in stores:
+        store.wait()
 
 
 def results(*arrays):
     hbm = pl.BlockSpec(memory_space=pltpu.HBM)
+    n = len(arrays)
     return pl.pallas_call(
         hand_over,
         out_shape=tuple(jax.ShapeDtypeStruct(a.shape, a.dtype) for a in arrays),
-        in_specs=[hbm] * len(arrays),
-        out_specs=(hbm,) * len(arrays),
-        scratch_shapes=[pltpu.SemaphoreType.DMA((len(arrays),))],
+        in_specs=[hbm] * n,
+        out_specs=(hbm,) * n,
+        scratch_shapes=[pltpu.VMEM(a.shape, a.dtype) for a in arrays] + [pltpu.SemaphoreType.DMA((n,))] * 2,
         compiler_params=pltpu.CompilerParams(vmem_limit_bytes=60 * 1024 * 1024),
     )(*arrays)
 

time: 151 us -> 98.2 us (0.65)
  Pallas kernels: 150 us -> 97.4 us
    pallas_call x1, Pallas kernels: 56.3 us -> 2.31 us  [results(): pl.pallas_call(hand_over, out_shape=tuple((jax.ShapeDtypeStruct(a.shape,...]
where the time goes in v5:
time: 98.2 us; the launch traced here: 98 us
  Pallas kernels  97.4 us (99%)
    pallas_call x1, Pallas kernels, exchange(): pl.pallas_call(functools.partial(kernel, plan), out_shape=(jax.ShapeDtype...  95.1 us
    pallas_call x1, Pallas kernels, results(): pl.pallas_call(hand_over, out_shape=tuple((jax.ShapeDtypeStruct(a.shape,...  2.31 us

profile of v5, /device:TPU:4, one launch (start us, length us, event | category | flops | bytes accessed | tf_op | source)
XLA Modules:
  0.0 98.0 jit_solution(5661856713308174338)
XLA Ops:
  0.6 95.1 %shard_map.144 = (bf16[64,384]{1,0:T(8,128)(2,1)}, bf16[384,384]{1,0:T(8,128)(2,1)}, bf16[384,384]{1,0:T(8,128)(2,1)}, bf16[384,384]{1,0:T(8,128)(2,1)}, bf16[38...) custom-call(bf16[64,384]{1,0:T(8,128)(2,1)} %og_ref.1, bf16[64,384]{1,0:T(8,128)(2,1)} %in_ref.1, ...), custom_call_target="tpu_custom_call" | custom-call | tf_op jit(solution)/shard_map/pallas_call | solution.py:651
  95.7 2.3 %shard_map.145 = (bf16[64,384]{1,0:T(8,128)(2,1)}, bf16[384,384]{1,0:T(8,128)(2,1)}, bf16[384,384]{1,0:T(8,128)(2,1)}, bf16[384,384]{1,0:T(8,128)(2,1)}, bf16[38...) custom-call(bf16[64,384]{1,0:T(8,128)(2,1)} %get-tuple-element.14.refs_0_, ...), custom_call_target="tpu_custom_call" | custom-call | tf_op jit(solution)/shard_map/pallas_call | solution.py:714

commit v6 on v5

--- a/solution.py
+++ b/solution.py
@@ -71,9 +71,9 @@
         self.FL = hidden
         self.subs_act, self.subs_rs, self.subs_del = 2, 4, 4
         self.act_1, self.act_2, self.act_3, self.act_every = 2, 2, 10, 2
-        self.lag1, self.lag2 = 3, 7
+        self.lag1, self.lag2 = 3, 6
         self.jump_rs, self.jump_del = 1, 1
-        self.lead, self.in_1, self.early, self.act_4 = 4, 2, 5, 11
+        self.lead, self.in_1, self.early, self.act_4 = 1, 2, 5, 11
         self.adam_rows = 32
         self.ops = 2
         self.call = 0
@@ -597,18 +597,15 @@
     loop(0, NZ, del_step)
     for get in get_adam:
         get.wait()
-    loop(NZ - LAG1, NZ - 1, pair)
-    blocks = plan.FL // ROWS
-    adam(wout, moments_out, seconds_out, gout_ref, 0, blocks // 2)
-    pair(NZ - 1)
+    loop(NZ - LAG1, NZ, pair)
     loop(NZ - LAG2, NZ - 1, line)
-    adam(wout, moments_out, seconds_out, gout_ref, blocks // 2, blocks)
+    adam(wout, moments_out, seconds_out, gout_ref, 0, plan.FL // ROWS)
     for put in put_out:
         put.start()
     blocks = plan.DL // ROWS
-    adam(win, moments_in, seconds_in, gin_ref, 0, blocks // 2)
+    adam(win, moments_in, seconds_in, gin_ref, 0, blocks // 4)
     line(NZ - 1)
-    adam(win, moments_in, seconds_in, gin_ref, blocks // 2, blocks)
+    adam(win, moments_in, seconds_in, gin_ref, blocks // 4, blocks)
     for put in put_in:
         put.start()
 

time: 98.2 us -> 96.8 us (0.986)
  Pallas kernels: 97.4 us -> 96.1 us
    pallas_call x1, Pallas kernels: 95.1 us -> 93.7 us  [exchange(): pl.pallas_call(functools.partial(kernel, plan), out_shape=(jax.ShapeDtype...]
where the time goes in v6:
time: 96.8 us; the launch traced here: 96.7 us
  Pallas kernels  96.1 us (99%)
    pallas_call x1, Pallas kernels, exchange(): pl.pallas_call(functools.partial(kernel, plan), out_shape=(jax.ShapeDtype...  93.7 us
    pallas_call x1, Pallas kernels, results(): pl.pallas_call(hand_over, out_shape=tuple((jax.ShapeDtypeStruct(a.shape,...  2.31 us

profile of v6, /device:TPU:4, one launch (start us, length us, event | category | flops | bytes accessed | tf_op | source)
XLA Modules:
  0.0 96.7 jit_solution(14295667502590376838)
XLA Ops:
  0.6 93.7 %shard_map.144 = (bf16[64,384]{1,0:T(8,128)(2,1)}, bf16[384,384]{1,0:T(8,128)(2,1)}, bf16[384,384]{1,0:T(8,128)(2,1)}, bf16[384,384]{1,0:T(8,128)(2,1)}, bf16[38...) custom-call(bf16[64,384]{1,0:T(8,128)(2,1)} %og_ref.1, bf16[64,384]{1,0:T(8,128)(2,1)} %in_ref.1, ...), custom_call_target="tpu_custom_call" | custom-call | tf_op jit(solution)/shard_map/pallas_call | solution.py:648
  94.4 2.3 %shard_map.145 = (bf16[64,384]{1,0:T(8,128)(2,1)}, bf16[384,384]{1,0:T(8,128)(2,1)}, bf16[384,384]{1,0:T(8,128)(2,1)}, bf16[384,384]{1,0:T(8,128)(2,1)}, bf16[38...) custom-call(bf16[64,384]{1,0:T(8,128)(2,1)} %get-tuple-element.14.refs_0_, ...), custom_call_target="tpu_custom_call" | custom-call | tf_op jit(solution)/shard_map/pallas_call | solution.py:711

commit v7 on v6

--- a/solution.py
+++ b/solution.py
@@ -69,7 +69,8 @@
         self.TB = 2 * tokens
         self.DL = features
         self.FL = hidden
-        self.subs_act, self.subs_rs, self.subs_del = 2, 4, 4
+        self.subs_act, self.subs_rs = 2, 4
+        self.subs_del = self.subs_rs
         self.act_1, self.act_2, self.act_3, self.act_every = 2, 2, 10, 2
         self.lag1, self.lag2 = 3, 6
         self.jump_rs, self.jump_del = 1, 1
@@ -200,11 +201,10 @@
             part = rows(self.buf, block * TB + sub * size, size)
             return remote(part, part, self.ssem, self.rsem.at[n, sub], plane(sign(n) * hops))
 
-        def start(self):
+        def start(self, sub):
             for dist in (1, self.jump) if self.jump > 1 else (1,):
                 for n in (2 * dist - 2, 2 * dist - 1):
-                    for sub in range(self.subs):
-                        self.copy(z, n, sub, dist).start()
+                    self.copy(z, n, sub, dist).start()
 
         def passed(self, n):
             block = mod(z - sign(n) * (div(n, 2) + 1) + 2 * NZ, NZ)
@@ -326,7 +326,8 @@
     get_pre.wait()
     act, slope = gelu_parts(pre[...])
     act_all[block] = act.astype(BF)
-    acts.start()
+    for sub in range(plan.subs_act):
+        acts.start(sub)
 
     @pl.when(late)
     def _():
@@ -440,14 +441,17 @@
             inp.third(x_peer(div(i, Y - 1) + 1), y_peer(mod(i, Y - 1) + 1))
 
     loop(0, NZ, rs_step)
-    total = ring[1, OWN].astype(F32)
-    for slot in (0, FAR) if JUMP > 1 else (FAR,):
-        for way in (0, 1):
-            for sub in range(plan.subs_rs):
+    size = TB // plan.subs_rs
+    for sub in range(plan.subs_rs):
+        here = pl.ds(sub * size, size)
+        total = ring[1, OWN, here].astype(F32)
+        for slot in (0, FAR) if JUMP > 1 else (FAR,):
+            for way in (0, 1):
                 rs_got(way, slot, sub).wait_recv()
-            total = total + ring[way, slot].astype(F32)
-    del_all[block] = (total * slopes[...]).astype(BF)
-    deltas.start()
+                total = total + ring[way, slot, here].astype(F32)
+        piece = pl.ds(pl.multiple_of(z * TB + sub * size, 16), size)
+        del_all[piece] = (total * slopes[here]).astype(BF)
+        deltas.start(sub)
     loop(0, X * Y, lambda i: inp.from_sib(div(i, Y), mod(i, Y)).wait_recv())
 
     def far(i):

time: 96.8 us -> 96 us (level)
  no operation moved by 1% of the time
where the time goes in v7:
time: 96 us; the launch traced here: 95.9 us
  Pallas kernels  95.2 us (99%)
    pallas_call x1, Pallas kernels, exchange(): pl.pallas_call(functools.partial(kernel, plan), out_shape=(jax.ShapeDtype...  92.9 us
    pallas_call x1, Pallas kernels, results(): pl.pallas_call(hand_over, out_shape=tuple((jax.ShapeDtypeStruct(a.shape,...  2.31 us

profile of v7, /device:TPU:4, one launch (start us, length us, event | category | flops | bytes accessed | tf_op | source)
XLA Modules:
  0.0 95.9 jit_solution(11241110426122754980)
XLA Ops:
  0.6 92.9 %shard_map.144 = (bf16[64,384]{1,0:T(8,128)(2,1)}, bf16[384,384]{1,0:T(8,128)(2,1)}, bf16[384,384]{1,0:T(8,128)(2,1)}, bf16[384,384]{1,0:T(8,128)(2,1)}, bf16[38...) custom-call(bf16[64,384]{1,0:T(8,128)(2,1)} %og_ref.1, bf16[64,384]{1,0:T(8,128)(2,1)} %in_ref.1, ...), custom_call_target="tpu_custom_call" | custom-call | tf_op jit(solution)/shard_map/pallas_call | solution.py:652
  93.5 2.3 %shard_map.145 = (bf16[64,384]{1,0:T(8,128)(2,1)}, bf16[384,384]{1,0:T(8,128)(2,1)}, bf16[384,384]{1,0:T(8,128)(2,1)}, bf16[384,384]{1,0:T(8,128)(2,1)}, bf16[38...) custom-call(bf16[64,384]{1,0:T(8,128)(2,1)} %get-tuple-element.14.refs_0_, ...), custom_call_target="tpu_custom_call" | custom-call | tf_op jit(solution)/shard_map/pallas_call | solution.py:715
